TPU v7x, 256 devices: a whole 4x4x8 slice. The times are simulated.
256 devices in a mesh: group: 64 (over y_lo, x, z), mp: 4 (over y_hi, core).
Axes of the slice: x: 4, y: 4 (y_hi: 2, y_lo: 2; y = y_hi * 2 + y_lo), z: 8, core: 2. Of those that a mesh axis runs over, the one named last changes fastest.
Arguments:
- tokens: bfloat16 [24576, 1024], P('group', 'mp'), may hold values from -6 to 6
- cotangent: bfloat16 [24576, 1024], P('group', 'mp'), may hold values from -6 to 6
- tags: int32 [24576], P('group'), may hold values from 0 to 2, as said below
- counts: int32 [3], replicated, may hold values from 384 to 12288, as said below
- target: int32 [24576], P('group'), may hold values from 0 to 31, as said below
- gate_weight: bfloat16 [3, 1024, 4096], P(None, 'group', 'mp'), may hold values from -0.1875 to 0.1875
- up_weight: bfloat16 [3, 1024, 4096], P(None, 'group', 'mp'), may hold values from -0.1875 to 0.1875
- down_weight: bfloat16 [3, 1024, 4096], P(None, 'group', 'mp'), may hold values from -0.09375 to 0.09375
Outputs:
- mixed: bfloat16 [24576, 1024], P('group', 'mp')
- token_grad: bfloat16 [24576, 1024], P('group', 'mp')
- gate_grad: float32 [3, 1024, 4096], P(None, 'group', 'mp')
- up_grad: float32 [3, 1024, 4096], P(None, 'group', 'mp')
- down_grad: float32 [3, 1024, 4096], P(None, 'group', 'mp')
Inputs may be any that keep to these rules, and one draw needn't show every extreme that they name: tags[t] is the modality of token t. counts[m] is the number of tokens tagged m and a multiple of 384; every modality is served by 1 to 32 devices, exactly one of them by 32. start[tags] + target lies in the range of devices that serve the token's modality; of the 384 tokens of one index of group at most 12 go to any one device, exactly 12 to some device in every owner and from some owner to every device; every device receives exactly 384 tokens in all.
All inputs are finite; a program needn't handle non-finite values.
Results may differ from a plain program's by a relative error of at most 0.005.
Values may be sent and summed in bfloat16 or wider, within the bound.
A program may use at most 128 MiB of HBM per device.

v0:
```python
import jax
import jax.numpy as jnp
from jax import lax
from jax.sharding import PartitionSpec as P


def project_rows(x, dy, wg, wu, wd):
    gate = jnp.dot(x, wg, preferred_element_type=jnp.float32)
    up = jnp.dot(x, wu, preferred_element_type=jnp.float32)
    sig = jax.nn.sigmoid(gate)
    silu = gate * sig
    hidden = (silu * up).astype(jnp.bfloat16)
    out = lax.dot_general(hidden, wd, (((1,), (1,)), ((), ())), preferred_element_type=jnp.float32)
    dhidden = jnp.dot(dy, wd, preferred_element_type=jnp.float32)
    dgate = (dhidden * up * sig * (1.0 + gate * (1.0 - sig))).astype(jnp.bfloat16)
    dup = (dhidden * silu).astype(jnp.bfloat16)
    dx = lax.dot_general(dgate, wg, (((1,), (1,)), ((), ())), preferred_element_type=jnp.float32)
    dx = dx + lax.dot_general(dup, wu, (((1,), (1,)), ((), ())), preferred_element_type=jnp.float32)
    grad_g = lax.dot_general(
        x, dgate, (((0,), (0,)), ((), ())), preferred_element_type=jnp.float32
    ).astype(jnp.bfloat16)
    grad_u = lax.dot_general(
        x, dup, (((0,), (0,)), ((), ())), preferred_element_type=jnp.float32
    ).astype(jnp.bfloat16)
    grad_d = lax.dot_general(
        dy, hidden, (((0,), (0,)), ((), ())), preferred_element_type=jnp.float32
    ).astype(jnp.bfloat16)
    return (out, dx, grad_g, grad_u, grad_d)


def choose_mod(mods, table):
    mask_zero = (mods == 0)[:, None, None]
    mask_one = (mods == 1)[:, None, None]
    return jnp.where(mask_zero, table[0][None], jnp.where(mask_one, table[1][None], table[2][None]))


def shards(tokens, cotangent, tags, counts, target, gate_weight, up_weight, down_weight):
    groups = lax.axis_size("group")
    rows = tokens.shape[0]
    feats = tokens.shape[1]
    slots = 2 * rows // groups
    total = rows * groups
    start_b = groups * counts[0] // total
    start_c = groups * (counts[0] + counts[1]) // total
    devices = jnp.arange(groups, dtype=jnp.int32)
    device_mod = (devices >= start_b).astype(jnp.int32) + (devices >= start_c).astype(jnp.int32)
    base = jnp.where(tags == 0, 0, jnp.where(tags == 1, start_b, start_c))
    dest = base + target
    onehot = (dest[:, None] == devices[None, :]).astype(jnp.float32)
    places = jnp.arange(rows, dtype=jnp.int32)
    lower = (places[:, None] > places[None, :]).astype(jnp.float32)
    earlier = jnp.dot(lower, onehot, precision=lax.Precision.HIGHEST)
    slot = jnp.sum(earlier * onehot, axis=1).astype(jnp.int32)
    position = dest * slots + slot
    empty = jnp.zeros((groups * slots, feats), jnp.bfloat16)
    send_x = empty.at[position].set(tokens)
    send_dy = empty.at[position].set(cotangent)
    pick_g = choose_mod(device_mod, gate_weight).reshape(-1, gate_weight.shape[2])
    pick_u = choose_mod(device_mod, up_weight).reshape(-1, up_weight.shape[2])
    pick_d = choose_mod(device_mod, down_weight).reshape(-1, down_weight.shape[2])
    w_gate, w_up, w_down = (
        lax.all_to_all(pick_g, "group", split_axis=0, concat_axis=0, tiled=True),
        lax.all_to_all(pick_u, "group", split_axis=0, concat_axis=0, tiled=True),
        lax.all_to_all(pick_d, "group", split_axis=0, concat_axis=0, tiled=True),
    )
    recv_x, recv_dy = (
        lax.all_to_all(send_x, "group", split_axis=0, concat_axis=0, tiled=True),
        lax.all_to_all(send_dy, "group", split_axis=0, concat_axis=0, tiled=True),
    )
    full_x, full_dy = (
        lax.all_gather(recv_x, "mp", axis=1, tiled=True),
        lax.all_gather(recv_dy, "mp", axis=1, tiled=True),
    )
    out_part, dx_part, grad_g, grad_u, grad_d = project_rows(full_x, full_dy, w_gate, w_up, w_down)
    out_sum, dx_sum = lax.psum((out_part, dx_part), "mp")
    offset = lax.axis_index("mp") * feats
    out_sum = lax.dynamic_slice_in_dim(out_sum, offset, feats, 1)
    dx_sum = lax.dynamic_slice_in_dim(dx_sum, offset, feats, 1)
    back_out, back_dx = (
        lax.all_to_all(
            out_sum.astype(jnp.bfloat16), "group", split_axis=0, concat_axis=0, tiled=True
        ),
        lax.all_to_all(
            dx_sum.astype(jnp.bfloat16), "group", split_axis=0, concat_axis=0, tiled=True
        ),
    )
    mixed = back_out[position]
    token_grad = back_dx[position]
    recv_g, recv_u, recv_d = (
        lax.all_to_all(grad_g, "group", split_axis=0, concat_axis=0, tiled=True),
        lax.all_to_all(grad_u, "group", split_axis=0, concat_axis=0, tiled=True),
        lax.all_to_all(grad_d, "group", split_axis=0, concat_axis=0, tiled=True),
    )
    block_rows = gate_weight.shape[1]
    width = gate_weight.shape[2]

    def by_modality(blocks):
        stacked = blocks.reshape(groups, block_rows, width).astype(jnp.float32)
        sums = [
            jnp.sum(jnp.where((device_mod == which)[:, None, None], stacked, 0.0), axis=0)
            for which in range(3)
        ]
        return jnp.stack(sums)

    return (mixed, token_grad, by_modality(recv_g), by_modality(recv_u), by_modality(recv_d))


def solution(mesh):
    in_specs = (
        P("group", "mp"),
        P("group", "mp"),
        P("group"),
        P(),
        P("group"),
        P(None, "group", "mp"),
        P(None, "group", "mp"),
        P(None, "group", "mp"),
    )
    out_specs = (
        P("group", "mp"),
        P("group", "mp"),
        P(None, "group", "mp"),
        P(None, "group", "mp"),
        P(None, "group", "mp"),
    )
    return jax.shard_map(shards, mesh=mesh, in_specs=in_specs, out_specs=out_specs, check_vma=False)
```

profile of v0, /device:TPU:16, one launch (start us, length us, event | category | flops | bytes accessed | tf_op | source)
XLA Modules:
  0.0 594.8 jit_solution(17156254349831956387)
XLA Ops:
  7.2 1.3 fusion.17
  10.5 0.7 select_add_fusion
  11.4 2.4 scatter_custom_fusion
  13.9 0.9 all_to_all.68
  14.7 12.7 %all-to-all-start = ((bf16[64,12,256]{2,1,0:T(8,128)(2,1)}), bf16[64,12,256]{2,1,0:T(8,128)(2,1)S(1)}, u32[]{:S(2)}, u32[]{:S(2)}) async-start(bf16[64,12,256]{2,1,0:T(8,128)(2,1)} %all_to_all.68), calls=%async_computation | async-start | bytes 1048576 | tf_op jit(solution)/shard_map/all_to_all | solution.py:67
  27.4 2.4 scatter_custom_fusion.1
  29.8 0.9 all_to_all.80
  30.7 15.4 %all-to-all-done = bf16[64,12,256]{2,1,0:T(8,128)(2,1)S(1)} async-done(((bf16[64,12,256]{2,1,0:T(8,128)(2,1)}), bf16[64,12,256]{2,1,0:T(8,128)(2,1)S(1)}, u32[]{:S(2)}, u32[]{:S(2)}) %all-to-all-start) | async-done | bytes 393248 | tf_op jit(solution)/shard_map/all_to_all | solution.py:67
  46.1 5.0 all-to-all-start.5
  51.2 2.5 select_select_fusion
  53.6 15.4 %all-to-all-done.5 = bf16[64,12,256]{2,1,0:T(8,128)(2,1)S(1)} async-done(((bf16[64,12,256]{2,1,0:T(8,128)(2,1)}), bf16[64,12,256]{2,1,0:T(8,128)(2,1)S(1)}, u32[]{:S(2)}, u32[]{:S(2)}) %all-to-all-start.5) | async-done | bytes 393248 | tf_op jit(solution)/shard_map/all_to_all | solution.py:68
  69.1 54.8 %all_to_all.102 = bf16[64,16,1024]{2,1,0:T(8,128)(2,1)} all-to-all(bf16[64,16,1024]{2,1,0:T(8,128)(2,1)S(1)} %get-tuple-element.35), channel_id=1, replica_groups=mesh['group'=64,'mp'=4] {'group'}, dimensions={0} | all-to-all | bytes 4194304 | tf_op jit(solution)/shard_map/all_to_all | solution.py:63
  123.9 6.0 %all-to-all-start.1 = ((bf16[64,16,1024]{2,1,0:T(8,128)(2,1)}), bf16[64,16,1024]{2,1,0:T(8,128)(2,1)S(1)}, u32[]{:S(2)}, u32[]{:S(2)}) async-start(bf16[64,16,1024]{2,1,0:T(8,128)(2,1)} %get-tuple-element.36), calls=%async_computation.1 | async-start | bytes 4194304 | tf_op jit(solution)/shard_map/all_to_all | solution.py:62
  130.0 0.8 all_to_all.70
  130.9 48.4 %all-to-all-done.1 = bf16[64,16,1024]{2,1,0:T(8,128)(2,1)S(1)} async-done(((bf16[64,16,1024]{2,1,0:T(8,128)(2,1)}), bf16[64,16,1024]{2,1,0:T(8,128)(2,1)S(1)}, u32[]{:S(2)}, u32[]{:S(2)}) %all-to-all-start.1) | async-done | bytes 2097184 | tf_op jit(solution)/shard_map/all_to_all | solution.py:62
  179.3 1.3 copy-done.2
  180.6 6.4 %all-to-all-start.3 = ((bf16[64,16,1024]{2,1,0:T(8,128)(2,1)}), bf16[64,16,1024]{2,1,0:T(8,128)(2,1)}, u32[]{:S(2)}, u32[]{:S(2)}) async-start(bf16[64,16,1024]{2,1,0:T(8,128)(2,1)} %get-tuple-element.34), calls=%async_computation.3 | async-start | bytes 4194304 | tf_op jit(solution)/shard_map/all_to_all | solution.py:64
  187.3 0.8 all_to_all.82
  188.2 5.0 fusion.19
  193.2 3.4 fusion.18
  196.7 25.0 %all-gather.5.cloned.1.call-done = bf16[768,1024]{1,0:T(8,128)(2,1)} async-done(((bf16[768,256]{1,0:T(8,128)(2,1)}), bf16[768,1024]{1,0:T(8,128)(2,1)}) %all-gather.5.cloned.1.call-update) | async-done | bytes 1572880 | tf_op jit(solution)/shard_map/all_gather | solution.py:72
  221.6 13.6 %all-to-all-done.3 = bf16[64,16,1024]{2,1,0:T(8,128)(2,1)} async-done(((bf16[64,16,1024]{2,1,0:T(8,128)(2,1)}), bf16[64,16,1024]{2,1,0:T(8,128)(2,1)}, u32[]{:S(2)}, u32[]{:S(2)}) %all-to-all-start.3) | async-done | bytes 2097184 | tf_op jit(solution)/shard_map/all_to_all | solution.py:64
  235.2 6.0 %multiply_convert_fusion = (bf16[768,1024]{1,0:T(8,128)(2,1)S(1)}, bf16[768,1024]{1,0:T(8,128)(2,1)S(1)}, bf16[768,1024]{1,0:T(8,128)(2,1)S(1)}) fusion(f32[768,1024]{1,0:T(8,128)} %fusion.18, f32[768,1024]{1,0:T(8,128)S(1)} %copy-done.10, bf16[768,1024]{1,0:T(8,128)(2,1)} %all-gather.5.cloned.1.call-done, bf16[1024,1024]{1,0:T(8,128)(2,1)} %bitcast.15), kind=kOutput, calls=%fused_computation.22 | convolution fusion | flops 1622409216 | bytes 14680064 | tf_op jit(solution)/shard_map/dot_general | solution.py:14
  241.3 1.8 fusion.21
  243.1 1.3 copy-done.1
  244.4 1.8 convolution_add_fusion
  246.3 5.1 fusion.20
  251.3 113.0 %all-reduce.2 = (bf16[768,1024]{1,0:T(8,128)(2,1)}, bf16[768,1024]{1,0:T(8,128)(2,1)}) all-reduce(f32[768,1024]{1,0:T(8,128)} %fusion.20, f32[768,1024]{1,0:T(8,128)S(1)} %convolution_add_fusion), channel_id=1, replica_groups=mesh['group'=64,'mp'=4] {'mp'}, use_global_device_ids=true, to_apply=%region_2.3 | all-reduce | flops 1572864 | bytes 9437184 | tf_op jit(solution)/shard_map/psum | solution.py:75
  364.3 1.0 dynamic-slice_convert_fusion
  365.3 0.9 all_to_all.83
  366.2 6.1 %all-to-all-start.6 = ((bf16[64,12,256]{2,1,0:T(8,128)(2,1)}), bf16[64,12,256]{2,1,0:T(8,128)(2,1)S(1)}, u32[]{:S(2)}, u32[]{:S(2)}) async-start(bf16[64,12,256]{2,1,0:T(8,128)(2,1)} %all_to_all.83), calls=%async_computation.6 | async-start | bytes 1048576 | tf_op jit(solution)/shard_map/all_to_all | solution.py:83
  372.3 1.0 dynamic-slice_convert_fusion.1
  373.3 0.9 all_to_all.77
  374.2 17.3 %all-to-all-done.6 = bf16[64,12,256]{2,1,0:T(8,128)(2,1)S(1)} async-done(((bf16[64,12,256]{2,1,0:T(8,128)(2,1)}), bf16[64,12,256]{2,1,0:T(8,128)(2,1)S(1)}, u32[]{:S(2)}, u32[]{:S(2)}) %all-to-all-start.6) | async-done | bytes 393248 | tf_op jit(solution)/shard_map/all_to_all | solution.py:83
  391.5 5.2 all-to-all-start.4
  396.8 4.6 convolution_convert_fusion.2
  401.3 13.6 %all-to-all-done.4 = bf16[64,12,256]{2,1,0:T(8,128)(2,1)S(1)} async-done(((bf16[64,12,256]{2,1,0:T(8,128)(2,1)}), bf16[64,12,256]{2,1,0:T(8,128)(2,1)S(1)}, u32[]{:S(2)}, u32[]{:S(2)}) %all-to-all-start.4) | async-done | bytes 393248 | tf_op jit(solution)/shard_map/all_to_all | solution.py:80
  414.9 5.0 all-to-all-start.7
  419.9 5.1 convolution_convert_fusion.1
  425.0 44.9 %all-to-all-done.7 = bf16[64,16,1024]{2,1,0:T(8,128)(2,1)S(1)} async-done(((bf16[64,16,1024]{2,1,0:T(8,128)(2,1)}), bf16[64,16,1024]{2,1,0:T(8,128)(2,1)S(1)}, u32[]{:S(2)}, u32[]{:S(2)}) %all-to-all-start.7) | async-done | bytes 2097184 | tf_op jit(solution)/shard_map/all_to_all | solution.py:90
  469.9 6.3 %all-to-all-start.8 = ((bf16[64,16,1024]{2,1,0:T(8,128)(2,1)}), bf16[64,16,1024]{2,1,0:T(8,128)(2,1)}, u32[]{:S(2)}, u32[]{:S(2)}) async-start(bf16[64,16,1024]{2,1,0:T(8,128)(2,1)} %bitcast.60), calls=%async_computation.8 | async-start | bytes 4194304 | tf_op jit(solution)/shard_map/all_to_all | solution.py:91
  476.2 5.0 convolution_convert_fusion
  481.2 44.1 %all-to-all-done.8 = bf16[64,16,1024]{2,1,0:T(8,128)(2,1)} async-done(((bf16[64,16,1024]{2,1,0:T(8,128)(2,1)}), bf16[64,16,1024]{2,1,0:T(8,128)(2,1)}, u32[]{:S(2)}, u32[]{:S(2)}) %all-to-all-start.8) | async-done | bytes 2097184 | tf_op jit(solution)/shard_map/all_to_all | solution.py:91
  525.4 6.6 %all-to-all-start.9 = ((bf16[64,16,1024]{2,1,0:T(8,128)(2,1)}), bf16[64,16,1024]{2,1,0:T(8,128)(2,1)}, u32[]{:S(2)}, u32[]{:S(2)}) async-start(bf16[64,16,1024]{2,1,0:T(8,128)(2,1)} %bitcast.59), calls=%async_computation.9 | async-start | bytes 4194304 | tf_op jit(solution)/shard_map/all_to_all | solution.py:92
  532.1 2.6 gather_fusion.1
  534.7 2.6 gather_fusion
  537.3 42.6 %all-to-all-done.9 = bf16[64,16,1024]{2,1,0:T(8,128)(2,1)} async-done(((bf16[64,16,1024]{2,1,0:T(8,128)(2,1)}), bf16[64,16,1024]{2,1,0:T(8,128)(2,1)}, u32[]{:S(2)}, u32[]{:S(2)}) %all-to-all-start.9) | async-done | bytes 2097184 | tf_op jit(solution)/shard_map/all_to_all | solution.py:92
  579.9 6.0 %fusion = (f32[16,1024]{1,0:T(8,128)S(1)}, f32[16,1024]{1,0:T(8,128)S(1)}, f32[16,1024]{1,0:T(8,128)S(1)}, f32[16,1024]{1,0:T(8,128)S(1)}, f32[16,1024]{1,0:T(8,...) fusion(bf16[64,16,1024]{2,1,0:T(8,128)(2,1)S(1)} %all-to-all-don, ...), kind=kLoop, calls=%fused_computation.13 | loop fusion | flops 21872640 | bytes 6881472 | tf_op jit(solution)/shard_map/reduce_sum | solution.py:100
  (43 shorter events, 2.9 us)
Async XLA Ops:
  7.2 23.5 %copy-start.5 = (bf16[3,16,1024]{2,1,0:T(8,128)(2,1)S(1)}, bf16[3,16,1024]{2,1,0:T(8,128)(2,1)}, u32[]{:S(2)}) copy-start(bf16[3,16,1024]{2,1,0:T(8,128)(2,1)} %param.13) | copy-start | bytes 294916
  13.8 37.3 %copy-start.6 = (bf16[3,16,1024]{2,1,0:T(8,128)(2,1)S(1)}, bf16[3,16,1024]{2,1,0:T(8,128)(2,1)}, u32[]{:S(2)}) copy-start(bf16[3,16,1024]{2,1,0:T(8,128)(2,1)} %param.15) | copy-start | bytes 294916
  13.8 37.3 %copy-start.7 = (bf16[3,16,1024]{2,1,0:T(8,128)(2,1)S(1)}, bf16[3,16,1024]{2,1,0:T(8,128)(2,1)}, u32[]{:S(2)}) copy-start(bf16[3,16,1024]{2,1,0:T(8,128)(2,1)} %param.14) | copy-start | bytes 294916
  14.7 31.4 %all-to-all-start = ((bf16[64,12,256]{2,1,0:T(8,128)(2,1)}), bf16[64,12,256]{2,1,0:T(8,128)(2,1)S(1)}, u32[]{:S(2)}, u32[]{:S(2)}) async-start(bf16[64,12,256]{2,1,0:T(8,128)(2,1)} %all_to_all.68), calls=%async_computation | async-start | bytes 1048576 | tf_op jit(solution)/shard_map/all_to_all | solution.py:67
  46.1 22.9 %all-to-all-start.5 = ((bf16[64,12,256]{2,1,0:T(8,128)(2,1)}), bf16[64,12,256]{2,1,0:T(8,128)(2,1)S(1)}, u32[]{:S(2)}, u32[]{:S(2)}) async-start(bf16[64,12,256]{2,1,0:T(8,128)(2,1)} %all_to_all.80), calls=%async_computation.5 | async-start | bytes 1048576 | tf_op jit(solution)/shard_map/all_to_all | solution.py:68
  123.9 55.3 %all-to-all-start.1 = ((bf16[64,16,1024]{2,1,0:T(8,128)(2,1)}), bf16[64,16,1024]{2,1,0:T(8,128)(2,1)S(1)}, u32[]{:S(2)}, u32[]{:S(2)}) async-start(bf16[64,16,1024]{2,1,0:T(8,128)(2,1)} %get-tuple-element.36), calls=%async_computation.1 | async-start | bytes 4194304 | tf_op jit(solution)/shard_map/all_to_all | solution.py:62
  130.0 58.2 %all-gather.3.cloned.1.call-start = ((), (), s32[]{:S(2)}) async-start(), calls=%async_computation.10 | async-start | bytes 1966080 | tf_op jit(solution)/shard_map/all_gather | solution.py:71
  179.3 1.3 copy-start.2
  180.6 7.6 %copy-start = (bf16[64,16,1024]{2,1,0:T(8,128)(2,1)S(1)}, bf16[64,16,1024]{2,1,0:T(8,128)(2,1)}, u32[]{:S(2)}) copy-start(bf16[64,16,1024]{2,1,0:T(8,128)(2,1)} %all_to_all.102) | copy-start | bytes 6291460
  180.6 54.6 %all-to-all-start.3 = ((bf16[64,16,1024]{2,1,0:T(8,128)(2,1)}), bf16[64,16,1024]{2,1,0:T(8,128)(2,1)}, u32[]{:S(2)}, u32[]{:S(2)}) async-start(bf16[64,16,1024]{2,1,0:T(8,128)(2,1)} %get-tuple-element.34), calls=%async_computation.3 | async-start | bytes 4194304 | tf_op jit(solution)/shard_map/all_to_all | solution.py:64
  187.0 34.6 %all-gather.5.cloned.1.call-start = ((), (), s32[]{:S(2)}) async-start(), calls=%async_computation.11 | async-start | bytes 1966080 | tf_op jit(solution)/shard_map/all_gather | solution.py:72
  188.2 5.1 copy-start.3
  188.2 5.1 copy-start.8
  193.2 42.0 %copy-start.10 = (f32[768,1024]{1,0:T(8,128)S(1)}, f32[768,1024]{1,0:T(8,128)}, u32[]{:S(2)}) copy-start(f32[768,1024]{1,0:T(8,128)} %fusion.19) | copy-start | bytes 9437188
  235.2 6.0 %copy-start.4 = (bf16[64,16,1024]{2,1,0:T(8,128)(2,1)S(1)}, bf16[64,16,1024]{2,1,0:T(8,128)(2,1)}, u32[]{:S(2)}) copy-start(bf16[64,16,1024]{2,1,0:T(8,128)(2,1)} %copy-done.2) | copy-start | bytes 6291460
  241.2 1.9 copy-start.13
  241.2 1.9 copy-start.11
  241.2 5.0 copy-start.12
  241.3 3.2 copy-start.1
  366.2 30.6 %copy-start.9 = (bf16[768,1024]{1,0:T(8,128)(2,1)S(1)}, bf16[768,1024]{1,0:T(8,128)(2,1)}, u32[]{:S(2)}) copy-start(bf16[768,1024]{1,0:T(8,128)(2,1)} %all-gather.3.cloned.1.call-done) | copy-start | bytes 4718596
  366.2 25.3 %all-to-all-start.6 = ((bf16[64,12,256]{2,1,0:T(8,128)(2,1)}), bf16[64,12,256]{2,1,0:T(8,128)(2,1)S(1)}, u32[]{:S(2)}, u32[]{:S(2)}) async-start(bf16[64,12,256]{2,1,0:T(8,128)(2,1)} %all_to_all.83), calls=%async_computation.6 | async-start | bytes 1048576 | tf_op jit(solution)/shard_map/all_to_all | solution.py:83
  391.5 23.4 %all-to-all-start.4 = ((bf16[64,12,256]{2,1,0:T(8,128)(2,1)}), bf16[64,12,256]{2,1,0:T(8,128)(2,1)S(1)}, u32[]{:S(2)}, u32[]{:S(2)}) async-start(bf16[64,12,256]{2,1,0:T(8,128)(2,1)} %all_to_all.77), calls=%async_computation.4 | async-start | bytes 1048576 | tf_op jit(solution)/shard_map/all_to_all | solution.py:80
  414.9 55.0 %all-to-all-start.7 = ((bf16[64,16,1024]{2,1,0:T(8,128)(2,1)}), bf16[64,16,1024]{2,1,0:T(8,128)(2,1)S(1)}, u32[]{:S(2)}, u32[]{:S(2)}) async-start(bf16[64,16,1024]{2,1,0:T(8,128)(2,1)} %bitcast.61), calls=%async_computation.7 | async-start | bytes 4194304 | tf_op jit(solution)/shard_map/all_to_all | solution.py:90
  469.9 55.5 %all-to-all-start.8 = ((bf16[64,16,1024]{2,1,0:T(8,128)(2,1)}), bf16[64,16,1024]{2,1,0:T(8,128)(2,1)}, u32[]{:S(2)}, u32[]{:S(2)}) async-start(bf16[64,16,1024]{2,1,0:T(8,128)(2,1)} %bitcast.60), calls=%async_computation.8 | async-start | bytes 4194304 | tf_op jit(solution)/shard_map/all_to_all | solution.py:91
  525.4 54.5 %all-to-all-start.9 = ((bf16[64,16,1024]{2,1,0:T(8,128)(2,1)}), bf16[64,16,1024]{2,1,0:T(8,128)(2,1)}, u32[]{:S(2)}, u32[]{:S(2)}) async-start(bf16[64,16,1024]{2,1,0:T(8,128)(2,1)} %bitcast.59), calls=%async_computation.9 | async-start | bytes 4194304 | tf_op jit(solution)/shard_map/all_to_all | solution.py:92
Sparse Core Ops, SparseCore 0:
  132.6 32.1 all-gather.2
  189.7 31.9 all-gather.4
where the time goes:
time: 597 us; the launch traced here: 595 us
  waiting for transfers between devices  280 us (47%)
  blocking collectives  168 us (28%)
  starting transfers between devices  59.5 us (10%)
  matrix products  38.1 us (6%)
  local copies, waits for them, and re-layouts  21.4 us (4%)
  between operations  16.4 us (3%)
  other arithmetic  11.3 us (2%)
    psum x1, blocking collectives, shards(): out_sum, dx_sum = lax.psum((out_part, dx_part), 'mp')  113 us
    all_to_all x1, blocking collectives, shards(): lax.all_to_all(pick_u, 'group', split_axis=0, concat_axis=0, tiled=True)  54.8 us
    all_to_all x1, waiting for transfers between devices, shards(): lax.all_to_all(pick_g, 'group', split_axis=0, concat_axis=0, tiled=True)  48.4 us
    all_to_all x1, waiting for transfers between devices, shards(): lax.all_to_all(grad_g, 'group', split_axis=0, concat_axis=0, tiled=True)  44.9 us
    all_to_all x1, waiting for transfers between devices, shards(): lax.all_to_all(grad_u, 'group', split_axis=0, concat_axis=0, tiled=True)  44.1 us
    all_to_all x1, waiting for transfers between devices, shards(): lax.all_to_all(grad_d, 'group', split_axis=0, concat_axis=0, tiled=True)  42.6 us
    all_gather x1, waiting for transfers between devices, shards(): lax.all_gather(recv_dy, 'mp', axis=1, tiled=True)  25 us
    all_to_all x1, waiting for transfers between devices, shards(): lax.all_to_all(dx_sum.astype(jnp.bfloat16), 'group', split_axis=0, concat...  17.3 us
  transfers between devices with their start and end apart: 11, of which 10 were waited for; matrix products, arithmetic and copies ran while one was open for 6% of the time, Pallas kernels for 0%

commit v1 on v0

v1 whole, which is shorter than its diff:
```python
import jax
import jax.numpy as jnp
from jax import lax
from jax.experimental import pallas as pl
from jax.experimental.pallas import tpu as pltpu
from jax.sharding import PartitionSpec as P

BF = jnp.bfloat16
F32 = jnp.float32
NX, NZ = 4, 8
HALF = NX * NZ
CAP = 12
SLOT = 16


def place():
    g = lax.axis_index("group")
    p = lax.axis_index("mp")
    h = lax.div(g, HALF)
    x = lax.rem(lax.div(g, NZ), NX)
    z = lax.rem(g, NZ)
    return p, h, x, z


def around(v, by, size):
    return lax.rem(v + (by + size), size)


def rows16(c):
    return pl.ds(pl.multiple_of(c * 16, 16), 16)


def greet(peers):
    barrier = pltpu.get_barrier_semaphore()
    for peer in peers:
        pl.semaphore_signal(barrier, inc=1, device_id=peer, device_id_type=pl.DeviceIdType.MESH)
    pl.semaphore_wait(barrier, len(peers))


def remote(src, dst, send, recv, peer):
    copy = pltpu.make_async_remote_copy(
        src_ref=src,
        dst_ref=dst,
        send_sem=send,
        recv_sem=recv,
        device_id=peer,
        device_id_type=pl.DeviceIdType.MESH,
    )
    copy.start()
    return copy


def gather_kernel(
    flags, wg, wu, wd, og, ou, od, zg, zu, zd, sbuf, relay, ys, yr, zs, zr, xs, xr, own
):
    p, h, x, z = place()

    def at(hh, xx, zz):
        return (hh * HALF + xx * NZ + zz, p)

    over = at(1 - h, x, z)
    zright, zleft = at(h, x, around(z, 1, NZ)), at(h, x, around(z, -1, NZ))
    xright, xleft = at(h, around(x, 1, NX), z), at(h, around(x, -1, NX), z)
    greet([over, zright, zleft, xright, xleft])
    weights = (wg, wu, wd)
    outs = (og, ou, od)
    zbuf = (zg, zu, zd)
    sends = []

    cross = []
    for w in range(3):
        cross.append(
            remote(
                weights[w].at[pl.ds(1 - h, 2)],
                zbuf[w].at[:, h, rows16(z), :],
                ys.at[w],
                yr.at[w],
                over,
            )
        )
        zbuf[w][:, h, rows16(z), :] = weights[w][pl.ds(h, 2)]

    def ring(w):
        cross[w].wait_recv()
        sends.append(cross[w])
        right = left = None
        for s in range(4):
            if s > 0:
                right.wait_recv()
                left.wait_recv()
            cr, cl = rows16(around(z, -s, NZ)), rows16(around(z, s, NZ))
            if s < 3:
                r, l = zbuf[w].at[:, :, cr, :], zbuf[w].at[:, :, cl, :]
            else:
                r, l = zbuf[w].at[:, 0, cr, :], zbuf[w].at[:, 1, cl, :]
            right = remote(r, r, zs.at[w, 0, s], zr.at[w, 0, s], zright)
            left = remote(l, l, zs.at[w, 1, s], zr.at[w, 1, s], zleft)
            sends.extend([right, left])
        right.wait_recv()
        left.wait_recv()

    waits = []
    far = {}

    def spread(w):
        for d in (2, 1, 3, 0):
            f = flags[h * HALF + around(x, d, NX) * NZ + z]
            sbuf[w, d] = zbuf[w][f]
            if d == 2:
                a = remote(sbuf.at[w, 2, 0], relay.at[w, 0], xs.at[w, 0], xr.at[w, 0], xright)
                b = remote(sbuf.at[w, 2, 1], relay.at[w, 1], xs.at[w, 1], xr.at[w, 1], xleft)
                far[w] = (a, b)
                sends.extend([a, b])
            elif d == 1:
                a = remote(sbuf.at[w, 1], outs[w].at[:, x], xs.at[w, 2], xr.at[w, 2], xright)
                sends.append(a)
                waits.append(a)
            elif d == 3:
                a = remote(sbuf.at[w, 3], outs[w].at[:, x], xs.at[w, 3], xr.at[w, 3], xleft)
                sends.append(a)
                waits.append(a)
            else:
                a = pltpu.make_async_copy(sbuf.at[w, 0], outs[w].at[:, x], own.at[w])
                a.start()
                far[w] = far[w] + (a,)

    def pass_on(w):
        a, b, c = far[w]
        a.wait_recv()
        r = remote(
            relay.at[w, 0],
            outs[w].at[0, around(x, -1, NX)],
            xs.at[w, 4],
            xr.at[w, 4],
            xright,
        )
        b.wait_recv()
        l = remote(
            relay.at[w, 1],
            outs[w].at[1, around(x, 1, NX)],
            xs.at[w, 5],
            xr.at[w, 5],
            xleft,
        )
        sends.extend([r, l])
        waits.extend([r, l])

    ring(0)
    spread(0)
    ring(1)
    pass_on(0)
    spread(1)
    ring(2)
    pass_on(1)
    spread(2)
    pass_on(2)
    for c in waits:
        c.wait_recv()
    for c in sends:
        c.wait_send()
    for w in range(3):
        far[w][2].wait()


def gather_weights(flags, wg, wu, wd):
    cols = wg.shape[2]
    vm = pl.BlockSpec(memory_space=pltpu.VMEM)
    dma = pltpu.SemaphoreType.DMA
    out = jax.ShapeDtypeStruct((2, NX, 16 * NZ, cols), BF)
    return pl.pallas_call(
        gather_kernel,
        out_shape=(out, out, out),
        in_specs=[pl.BlockSpec(memory_space=pltpu.SMEM), vm, vm, vm],
        out_specs=[pl.BlockSpec(memory_space=pl.ANY)] * 3,
        scratch_shapes=[
            pltpu.VMEM((2, 2, 16 * NZ, cols), BF),
            pltpu.VMEM((2, 2, 16 * NZ, cols), BF),
            pltpu.VMEM((2, 2, 16 * NZ, cols), BF),
            pltpu.VMEM((3, 4, 2, 16 * NZ, cols), BF),
            pltpu.VMEM((3, 2, 16 * NZ, cols), BF),
            dma((3,)),
            dma((3,)),
            dma((3, 2, 4)),
            dma((3, 2, 4)),
            dma((3, 6)),
            dma((3, 6)),
            dma((3,)),
        ],
        compiler_params=pltpu.CompilerParams(
            collective_id=0, has_side_effects=True, vmem_limit_bytes=48 * 1024 * 1024
        ),
        cost_estimate=pl.CostEstimate(flops=0, bytes_accessed=200_000_000, transcendentals=0),
        name="gather_weights",
    )(flags, wg, wu, wd)


def reduce_kernel(
    flags,
    gg,
    gu,
    gd,
    og,
    ou,
    od,
    rbuf,
    relay,
    zsum,
    zin,
    keep,
    ysend,
    yin,
    ys,
    yr,
    zs,
    zr,
    xs,
    xr,
    own,
):
    p, h, x, z = place()

    def at(hh, xx, zz):
        return (hh * HALF + xx * NZ + zz, p)

    over = at(1 - h, x, z)
    zright, zleft = at(h, x, around(z, 1, NZ)), at(h, x, around(z, -1, NZ))
    xr1, xl1 = around(x, 1, NX), around(x, -1, NX)
    xright, xleft = at(h, xr1, z), at(h, xl1, z)
    greet([over, zright, zleft, xright, xleft])
    grads = (gg, gu, gd)
    outs = (og, ou, od)
    sends = []
    first = {}

    def spread(w):
        g = grads[w]
        x2 = around(x, 2, NX)
        a = remote(g.at[0, x2], relay.at[w, 0], xs.at[w, 0], xr.at[w, 0], xright)
        b = remote(g.at[1, x2], relay.at[w, 1], xs.at[w, 1], xr.at[w, 1], xleft)
        c = remote(g.at[:, xr1], rbuf.at[w, 1], xs.at[w, 2], xr.at[w, 2], xright)
        d = remote(g.at[:, xl1], rbuf.at[w, 3], xs.at[w, 3], xr.at[w, 3], xleft)
        e = pltpu.make_async_copy(g.at[:, x], rbuf.at[w, 0], own.at[w])
        e.start()
        sends.extend([a, b, c, d])
        first[w] = (a, b, c, d, e)

    def pass_on(w):
        a, b, c, d, e = first[w]
        a.wait_recv()
        r = remote(relay.at[w, 0], rbuf.at[w, 2, 0], xs.at[w, 4], xr.at[w, 4], xright)
        b.wait_recv()
        l = remote(relay.at[w, 1], rbuf.at[w, 2, 1], xs.at[w, 5], xr.at[w, 5], xleft)
        sends.extend([r, l])
        first[w] = (c, d, r, l, e)

    def bins(w):
        c, d, r, l, e = first[w]
        e.wait()
        c.wait_recv()
        d.wait_recv()
        r.wait_recv()
        l.wait_recv()
        marks = [
            flags[h * HALF + around(x, by, NX) * NZ + z].astype(F32) for by in (0, -1, 2, 1)
        ]

        def body(i, _):
            y = lax.div(i, NZ)
            at_rows = rows16(lax.rem(i, NZ))
            low = high = None
            for k in range(4):
                v = rbuf[w, k, y, at_rows, :].astype(F32)
                b = v * marks[k]
                a = v - b
                low = a if low is None else low + a
                high = b if high is None else high + b
            zsum[w, 0, y, at_rows, :] = low.astype(BF)
            zsum[w, 1, y, at_rows, :] = high.astype(BF)
            return 0

        lax.fori_loop(0, 2 * NZ, body, 0)

    steps = {}

    def plus(a, b):
        return (a.astype(F32) + b.astype(F32)).astype(BF)

    def ring(w, s):
        for way, (peer, sign) in enumerate(((zright, 1), (zleft, -1))):
            part = rows16(around(z, sign * (4 - s), NZ))
            if s == 0:
                c = remote(
                    zsum.at[w, :, way, part, :],
                    zin.at[w, way, 0, :, way],
                    zs.at[w, way, 0],
                    zr.at[w, way, 0],
                    peer,
                )
            else:
                steps[w, way].wait_recv()
                if s == 1:
                    zin[w, way, 0, :, way] = plus(
                        zin[w, way, 0, :, way], zsum[w, :, way, part, :]
                    )
                    zin[w, way, 0, :, 1 - way] = zsum[w, :, 1 - way, part, :]
                else:
                    zin[w, way, s - 1] = plus(zin[w, way, s - 1], zsum[w, :, :, part, :])
                c = remote(
                    zin.at[w, way, s - 1],
                    zin.at[w, way, s],
                    zs.at[w, way, s],
                    zr.at[w, way, s],
                    peer,
                )
            steps[w, way] = c
            sends.append(c)

    cross = {}

    def total(w, y):
        part = rows16(z)
        v = zsum[w, :, y, part, :].astype(F32)
        v = v + zin[w, 0, 3, :, y].astype(F32)
        return v + zin[w, 1, 3, :, y].astype(F32)

    def swap(w):
        steps[w, 0].wait_recv()
        steps[w, 1].wait_recv()
        ysend[w] = total(w, 1 - h).astype(BF)
        cross[w] = remote(ysend.at[w], yin.at[w], ys.at[w], yr.at[w], over)
        sends.append(cross[w])
        keep[w] = total(w, h)

    def finish(w):
        cross[w].wait_recv()
        out = outs[w]
        out[2 * h] = keep[w, h]
        out[1] = keep[w, 1 - h] + yin[w, h].astype(F32)
        out[2 - 2 * h] = yin[w, 1 - h].astype(F32)

    for w in range(3):
        spread(w)
    for w in range(3):
        pass_on(w)
        bins(w)
        if w > 0:
            for s in range(2, 4):
                ring(w - 1, s)
        for s in range(2):
            ring(w, s)
        if w > 0:
            swap(w - 1)
    for s in range(2, 4):
        ring(2, s)
    swap(2)
    for w in range(3):
        finish(w)
    for c in sends:
        c.wait_send()


def reduce_grads(flags, gg, gu, gd):
    cols = gg.shape[1]
    shape = (2, NX, 16 * NZ, cols)
    vm = pl.BlockSpec(memory_space=pltpu.VMEM)
    dma = pltpu.SemaphoreType.DMA
    out = jax.ShapeDtypeStruct((3, 16, cols), F32)
    return pl.pallas_call(
        reduce_kernel,
        out_shape=(out, out, out),
        in_specs=[pl.BlockSpec(memory_space=pltpu.SMEM)]
        + [pl.BlockSpec(memory_space=pl.ANY)] * 3,
        out_specs=[vm] * 3,
        scratch_shapes=[
            pltpu.VMEM((3, 4, 2, 16 * NZ, cols), BF),
            pltpu.VMEM((3, 2, 16 * NZ, cols), BF),
            pltpu.VMEM((3, 2, 2, 16 * NZ, cols), BF),
            pltpu.VMEM((3, 2, 4, 2, 2, 16, cols), BF),
            pltpu.VMEM((3, 2, 16, cols), F32),
            pltpu.VMEM((3, 2, 16, cols), BF),
            pltpu.VMEM((3, 2, 16, cols), BF),
            dma((3,)),
            dma((3,)),
            dma((3, 2, 4)),
            dma((3, 2, 4)),
            dma((3, 6)),
            dma((3, 6)),
            dma((3,)),
        ],
        compiler_params=pltpu.CompilerParams(
            collective_id=1, has_side_effects=True, vmem_limit_bytes=48 * 1024 * 1024
        ),
        cost_estimate=pl.CostEstimate(flops=0, bytes_accessed=200_000_000, transcendentals=0),
        name="reduce_grads",
    )(flags, gg.reshape(shape), gu.reshape(shape), gd.reshape(shape))


def project_rows(x, dy, wg, wu, wd):
    gate = jnp.dot(x, wg, preferred_element_type=F32)
    up = jnp.dot(x, wu, preferred_element_type=F32)
    sig = jax.nn.sigmoid(gate)
    silu = gate * sig
    hidden = (silu * up).astype(BF)
    out = lax.dot_general(hidden, wd, (((1,), (1,)), ((), ())), preferred_element_type=F32)
    dhidden = jnp.dot(dy, wd, preferred_element_type=F32)
    dgate = (dhidden * up * sig * (1.0 + gate * (1.0 - sig))).astype(BF)
    dup = (dhidden * silu).astype(BF)
    dx = lax.dot_general(dgate, wg, (((1,), (1,)), ((), ())), preferred_element_type=F32)
    dx = dx + lax.dot_general(dup, wu, (((1,), (1,)), ((), ())), preferred_element_type=F32)
    over_rows = (((0,), (0,)), ((), ()))
    grad_g = lax.dot_general(x, dgate, over_rows, preferred_element_type=F32).astype(BF)
    grad_u = lax.dot_general(x, dup, over_rows, preferred_element_type=F32).astype(BF)
    grad_d = lax.dot_general(dy, hidden, over_rows, preferred_element_type=F32).astype(BF)
    return out, dx, grad_g, grad_u, grad_d


def pick(onehot, rows):
    return jnp.dot(onehot, rows, preferred_element_type=F32).astype(BF)


def shards(tokens, cotangent, tags, counts, target, gate_weight, up_weight, down_weight):
    groups = lax.axis_size("group")
    parts = lax.axis_size("mp")
    rows, feats = tokens.shape
    total = rows * groups
    start_b = groups * counts[0] // total
    start_c = groups * (counts[0] + counts[1]) // total
    devices = jnp.arange(groups, dtype=jnp.int32)
    device_mod = (devices >= start_b).astype(jnp.int32) + (devices >= start_c).astype(jnp.int32)
    flags = device_mod - devices // HALF
    base = jnp.where(tags == 0, 0, jnp.where(tags == 1, start_b, start_c))
    dest = base + target
    onehot = (dest[:, None] == devices[None, :]).astype(BF)
    places = jnp.arange(rows, dtype=jnp.int32)
    lower = (places[:, None] > places[None, :]).astype(BF)
    earlier = jnp.dot(lower, onehot, preferred_element_type=F32)
    slot = jnp.sum(earlier * onehot.astype(F32), axis=1).astype(jnp.int32)
    sent = jnp.sum(onehot.astype(F32), axis=0)
    position = dest * SLOT + slot
    wide = groups * SLOT
    lanes = jnp.arange(wide, dtype=jnp.int32)
    both = jnp.concatenate([tokens, cotangent], axis=1)
    into = (lanes[:, None] == position[None, :]).astype(BF)
    send = jnp.dot(into, both, preferred_element_type=F32).reshape(groups, SLOT, 2 * feats)
    tail = (jnp.arange(SLOT, dtype=jnp.int32) >= CAP)[None, :, None]
    send = jnp.where(tail, sent[:, None, None], send).astype(BF).reshape(wide, 2 * feats)
    recv = lax.all_to_all(send, "group", split_axis=0, concat_axis=0, tiled=True)
    got = recv.reshape(groups, SLOT, 2 * feats)[:, CAP, 0].astype(jnp.int32)
    before = jnp.sum(jnp.where(devices[:, None] > devices[None, :], got[None, :], 0), axis=1)
    spot = jnp.arange(SLOT, dtype=jnp.int32)[None, :]
    rank = jnp.where(spot < got[:, None], before[:, None] + spot, -1).reshape(wide)
    close = (places[:, None] == rank[None, :]).astype(BF)
    open_up = (rank[:, None] == places[None, :]).astype(BF)
    mine = pick(close, recv)
    full = lax.all_gather(mine, "mp", axis=0, tiled=False)
    full = full.transpose(1, 0, 2)
    full_x = full[:, :, :feats].reshape(rows, parts * feats)
    full_dy = full[:, :, feats:].reshape(rows, parts * feats)
    w_gate, w_up, w_down = gather_weights(flags, gate_weight, up_weight, down_weight)
    depth = parts * feats
    w_gate, w_up, w_down = (w.reshape(depth, -1) for w in (w_gate, w_up, w_down))
    out, dx, grad_g, grad_u, grad_d = project_rows(full_x, full_dy, w_gate, w_up, w_down)
    pieces = jnp.concatenate(
        [out.reshape(rows, parts, feats), dx.reshape(rows, parts, feats)], axis=2
    )
    pieces = pieces.astype(BF).transpose(1, 0, 2)
    pieces = lax.all_to_all(pieces, "mp", split_axis=0, concat_axis=0, tiled=True)
    summed = jnp.sum(pieces.astype(F32), axis=0).astype(BF)
    back = pick(open_up, summed)
    back = lax.all_to_all(back, "group", split_axis=0, concat_axis=0, tiled=True)
    result = pick(into.T, back)
    mixed, token_grad = result[:, :feats], result[:, feats:]
    gate_grad, up_grad, down_grad = reduce_grads(flags, grad_g, grad_u, grad_d)
    return mixed, token_grad, gate_grad, up_grad, down_grad


def solution(mesh):
    in_specs = (
        P("group", "mp"),
        P("group", "mp"),
        P("group"),
        P(),
        P("group"),
        P(None, "group", "mp"),
        P(None, "group", "mp"),
        P(None, "group", "mp"),
    )
    out_specs = (
        P("group", "mp"),
        P("group", "mp"),
        P(None, "group", "mp"),
        P(None, "group", "mp"),
        P(None, "group", "mp"),
    )
    return jax.shard_map(shards, mesh=mesh, in_specs=in_specs, out_specs=out_specs, check_vma=False)
```

time: 597 us -> 347 us (0.58)
  waiting for transfers between devices: 280 us -> 0.02 us
  Pallas kernels: 0 us -> 221 us
  blocking collectives: 168 us -> 65 us
  starting transfers between devices: 59.5 us -> 7.63 us
  matrix products: 38.1 us -> 21.7 us
  local copies, waits for them, and re-layouts: 21.4 us -> 11.8 us
  other arithmetic: 11.3 us -> 2.89 us
    all_to_all x9 -> x1, waiting for transfers between devices: 255 us -> 0.01 us  [shards(): lax.all_to_all(back, 'group', split_axis=0, concat_axis=0, tiled=True)]
    pallas_call x0 -> x2, Pallas kernels: none -> 221 us  [the longest x1 131 us: reduce_grads(): pl.pallas_call(reduce_kernel, out_shape=(out, out, out), in_specs=[pl.Blo...]
    psum x1 -> x0, blocking collectives: 113 us -> none  [shards(): out_sum, dx_sum = lax.psum((out_part, dx_part), 'mp')]
    all_to_all x9 -> x1, starting transfers between devices: 59.2 us -> 7.59 us  [shards(): lax.all_to_all(back, 'group', split_axis=0, concat_axis=0, tiled=True)]
    all_gather x2 -> x1, waiting for transfers between devices: 25 us -> 0.01 us  [shards(): full = lax.all_gather(mine, 'mp', axis=0, tiled=False)]
    dot_general x7 -> x11, matrix products: 29.4 us -> 16.5 us  [the longest x1 3.81 us: project_rows(): lax.dot_general(dy, hidden, over_rows, preferred_element_type=F32)]
    all_to_all x1 -> x2, blocking collectives: 54.8 us -> 65 us  [the longest x1 42 us: shards(): lax.all_to_all(send, 'group', split_axis=0, concat_axis=0, tiled=True)]
  transfers between devices with their start and end apart: 11 -> 2, of which waited for: 10 -> 0; matrix products, arithmetic and copies ran while one was open for 6% -> 2% of each run, Pallas kernels for 0% -> 64%
where the time goes in v1:
time: 347 us; the launch traced here: 346 us
  Pallas kernels  221 us (64%)
  blocking collectives  65 us (19%)
  matrix products  21.7 us (6%)
  between operations  16.3 us (5%)
  local copies, waits for them, and re-layouts  11.8 us (3%)
  starting transfers between devices  7.63 us (2%)
    pallas_call x1, Pallas kernels, reduce_grads(): pl.pallas_call(reduce_kernel, out_shape=(out, out, out), in_specs=[pl.Blo...  131 us
    pallas_call x1, Pallas kernels, gather_weights(): pl.pallas_call(gather_kernel, out_shape=(out, out, out), in_specs=[pl.Blo...  90.5 us
    all_to_all x1, blocking collectives, shards(): lax.all_to_all(send, 'group', split_axis=0, concat_axis=0, tiled=True)  42 us
    all_to_all x1, blocking collectives, shards(): lax.all_to_all(pieces, 'mp', split_axis=0, concat_axis=0, tiled=True)  23 us
    all_to_all x1, starting transfers between devices, shards(): lax.all_to_all(back, 'group', split_axis=0, concat_axis=0, tiled=True)  7.59 us
  transfers between devices with their start and end apart: 2, of which 0 were waited for; matrix products, arithmetic and copies ran while one was open for 2% of the time, Pallas kernels for 64%

profile of v1, /device:TPU:16, one launch (start us, length us, event | category | flops | bytes accessed | tf_op | source)
XLA Modules:
  0.0 346.5 jit_solution(5838817555378175156)
XLA Ops:
  7.2 0.0 all-gather.3.cloned.1.call-start
  7.2 1.3 fusion.24
  10.5 0.7 select_add_fusion
  11.3 0.1 convert_reduce_fusion
  11.4 0.2 fusion.7
  11.6 0.1 broadcast_in_dim.69
  11.7 0.1 broadcast_in_dim.71
  11.8 0.1 broadcast_in_dim.72
  11.9 1.7 select_convert_fusion
  13.6 42.0 %all_to_all.29 = bf16[64,16,512]{2,1,0:T(8,128)(2,1)S(1)} all-to-all(bf16[64,16,512]{2,1,0:T(8,128)(2,1)S(1)} %bitcast.66), channel_id=1, replica_groups=mesh['group'=64,'mp'=4] {'group'}, dimensions={0} | all-to-all | bytes 2097152 | tf_op jit(solution)/shard_map/all_to_all | solution.py:447
  55.6 1.2 fusion.18
  56.9 0.1 select_reduce_fusion
  57.0 0.1 add_select_fusion
  57.1 0.1 select_n.52
  57.1 1.3 fusion.5
  58.5 0.0 all-gather.3.cloned.1.call-update
  58.6 90.5 %gather_weights.1 = (bf16[2,4,128,1024]{3,2,1,0:T(8,128)(2,1)S(1)}, bf16[2,4,128,1024]{3,2,1,0:T(8,128)(2,1)S(1)}, bf16[2,4,128,1024]{3,2,1,0:T(8,128)(2,1)}) custom-call(s32[64]{0:T(128)S(1)} %fusion.19.flags, bf16[3,16,1024]{2,1,0:T(8,128)(2,1)S(1)} %copy-done, bf16[3,16,1024]{2,1,0:T(8,128)(2,1)S(1)} %copy-done.1, bf16[3,16,1024]{2,1,0:T(8,128)(2,1)S(1)} %copy-done.2), custom_call_target="tpu_custom_call" | custom-call | bytes 200000000 | tf_op jit(solution)/shard_map/gather_weights/pallas_call | solution.py:170
  149.1 1.3 copy-done.3
  150.4 2.6 copy.19
  153.0 1.5 fusion.22
  154.5 1.0 fusion.25
  155.5 0.9 copy-done.7
  156.4 1.0 fusion.26
  157.4 0.6 copy-done.4
  158.0 2.5 multiply_convert_fusion.2
  160.5 1.0 fusion.27
  161.6 0.0 copy-done.10
  161.6 0.1 copy-done.8
  161.7 1.0 add_convert_fusion
  162.7 0.4 copy.20
  163.1 3.1 convolution_convert_fusion.3
  166.2 0.2 maximum_bitcast_fusion
  166.4 23.0 %all_to_all.30 = bf16[4,384,512]{1,2,0:T(8,128)(2,1)S(1)} all-to-all(bf16[4,384,512]{1,2,0:T(8,128)(2,1)S(1)} %maximum_bitcast_fusion), channel_id=1, replica_groups=mesh['group'=64,'mp'=4] {'mp'}, dimensions={0} | all-to-all | bytes 3145728 | tf_op jit(solution)/shard_map/all_to_all | solution.py:467
  189.4 0.4 reduce_sum.42
  189.8 1.7 fusion.4
  191.6 7.6 %all-to-all-start.2 = ((bf16[64,16,512]{2,1,0:T(8,128)(2,1)}), bf16[64,16,512]{2,1,0:T(8,128)(2,1)S(1)}, u32[]{:S(2)}, u32[]{:S(2)}) async-start(bf16[64,16,512]{2,1,0:T(8,128)(2,1)} %bitcast.65), calls=%async_computation.2 | async-start | bytes 2097152 | tf_op jit(solution)/shard_map/all_to_all | solution.py:470
  199.2 0.0 copy-done.6
  199.2 0.0 copy-start.11
  199.2 3.8 %convolution_convert_fusion = bf16[1024,1024]{1,0:T(8,128)(2,1)} fusion(bf16[384,1024]{0,1:T(8,128)(2,1)S(1)} %bitcast.58, bf16[384,1024]{1,0:T(8,128)(2,1)} %get-tuple-element.17), kind=kOutput, calls=%fused_computation.1 | convolution fusion | flops 806354944 | bytes 3670016 | tf_op jit(solution)/shard_map/dot_general | solution.py:413
  203.0 1.3 convolution_convert_fusion.2
  204.3 1.2 convolution_convert_fusion.1
  205.5 130.7 %reduce_grads.1 = (f32[3,16,1024]{2,1,0:T(8,128)S(1)}, f32[3,16,1024]{2,1,0:T(8,128)S(1)}, f32[3,16,1024]{2,1,0:T(8,128)S(1)}) custom-call(s32[64]{0:T(128)S(1)} %fusion.19.flags, bf16[2,4,128,1024]{3,2,1,0:T(8,128)(2,1)S(1)} %bitcast.45, bf16[2,4,128,1024]{3,2,1,0:T(8,128)(2,1)S(1)} %bitcast.46, bf16[2,4,128,1024]{3,2,1,0:T(8,128)(2,1)} %bitcast.59), custom_call_target="tpu_custom_call" | custom-call | bytes 200000000 | tf_op jit(solution)/shard_map/reduce_grads/pallas_call | solution.py:368
  336.2 0.0 all-to-all-done.2
  336.2 0.6 fusion.6
  336.8 0.8 fusion.23
  337.6 0.7 copy.24
  338.3 0.7 copy.25
  339.0 0.7 copy.26
  (22 shorter events, 0.1 us)
Async XLA Ops:
  7.2 143.2 %all-gather.3.cloned.1.call-start = ((), (), s32[]{:S(2)}) async-start(), calls=%async_computation.3 | async-start | bytes 1966080 | tf_op jit(solution)/shard_map/all_gather | solution.py:455
  55.6 2.9 copy-start
  55.6 2.9 copy-start.1
  55.6 2.9 copy-start.2
  149.1 1.3 copy-start.3
  154.5 1.0 copy-start.5
  154.5 1.9 copy-start.7
  156.4 1.6 copy-start.4
  160.5 1.1 copy-start.10
  160.5 1.2 copy-start.8
  189.8 9.4 %copy-start.6 = (bf16[384,4,256]{0,2,1:T(8,128)(2,1)S(1)}, bf16[384,4,256]{0,2,1:T(8,128)(2,1)}, u32[]{:S(2)}) copy-start(bf16[384,4,256]{0,2,1:T(8,128)(2,1)} %copy-done.5) | copy-start | bytes 2359300
  191.6 144.6 %all-to-all-start.2 = ((bf16[64,16,512]{2,1,0:T(8,128)(2,1)}), bf16[64,16,512]{2,1,0:T(8,128)(2,1)S(1)}, u32[]{:S(2)}, u32[]{:S(2)}) async-start(bf16[64,16,512]{2,1,0:T(8,128)(2,1)} %bitcast.65), calls=%async_computation.2 | async-start | bytes 2097152 | tf_op jit(solution)/shard_map/all_to_all | solution.py:470
  199.2 3.8 %copy-start.11 = (bf16[384,1024]{1,0:T(8,128)(2,1)S(1)}, bf16[384,1024]{1,0:T(8,128)(2,1)}, u32[]{:S(2)}) copy-start(bf16[384,1024]{1,0:T(8,128)(2,1)} %copy-done.10) | copy-start | bytes 2359300
  203.0 1.3 copy-start.9
Sparse Core Ops, SparseCore 0:
  58.6 19.7 all-gather.2

commit v2 on v0

v2 whole, which is shorter than its diff:
```python
import jax
import jax.numpy as jnp
from jax import lax
from jax.experimental import pallas as pl
from jax.experimental.pallas import tpu as pltpu
from jax.sharding import PartitionSpec as P

BF = jnp.bfloat16
F32 = jnp.float32
NX, NZ = 4, 8
HALF = NX * NZ
CAP = 12
SLOT = 16
SPLIT = 2
HOOKS = (1, 6, 9, 12, 1, 3)


def place():
    g = lax.axis_index("group")
    p = lax.axis_index("mp")
    h = lax.div(g, HALF)
    x = lax.rem(lax.div(g, NZ), NX)
    z = lax.rem(g, NZ)
    return p, h, x, z


def around(v, by, size):
    return lax.rem(v + (by + size), size)


def rows16(c):
    return pl.ds(pl.multiple_of(c * 16, 16), 16)


def greet(peers):
    barrier = pltpu.get_barrier_semaphore()
    for peer in peers:
        pl.semaphore_signal(barrier, inc=1, device_id=peer, device_id_type=pl.DeviceIdType.MESH)
    pl.semaphore_wait(barrier, len(peers))


def remote(src, dst, send, recv, peer):
    copy = pltpu.make_async_remote_copy(
        src_ref=src,
        dst_ref=dst,
        send_sem=send,
        recv_sem=recv,
        device_id=peer,
        device_id_type=pl.DeviceIdType.MESH,
    )
    copy.start()
    return copy


def units(cols):
    wide = cols // SPLIT
    return [(w, pl.ds(i * wide, wide)) for w in range(3) for i in range(SPLIT)]


def peers_of(p, h, x, z):
    def at(hh, xx, zz):
        return (hh * HALF + xx * NZ + zz, p)

    zline = [at(h, x, around(z, d, NZ)) for d in range(1, NZ)]
    yx = h * NX + x
    plane = []
    for d in range(1, 2 * NX):
        k = around(yx, d, 2 * NX)
        plane.append((k, at(lax.div(k, NX), lax.rem(k, NX), z)))
    g = h * HALF + x * NZ + z
    core = p + 1 - 2 * lax.rem(p, 2)
    opposite = around(p, 2, 4)
    both = around(core, 2, 4)
    parts = [(core, (g, core)), (opposite, (g, opposite)), (both, (g, both))]
    return at, zline, plane, parts


def lanes_of(p, feats):
    return pl.ds(pl.multiple_of(p * feats, 128), feats)


def gather_kernel(flags, wg, wu, wd, tok, og, ou, od, fx, fdy, close, *scratch):
    n = 3 * SPLIT
    zbuf = scratch[:n]
    sbuf, relay, tmid, rows, mine = scratch[n : n + 5]
    ys, yr, zs, zr, xs, xr, own, ts, tr, tl, ms, mr, ml = scratch[n + 5 :]
    p, h, x, z = place()
    at, zline, plane, parts = peers_of(p, h, x, z)
    over = at(1 - h, x, z)
    zright, zleft = at(h, x, around(z, 1, NZ)), at(h, x, around(z, -1, NZ))
    xright, xleft = at(h, around(x, 1, NX), z), at(h, around(x, -1, NX), z)
    greet(zline + [q for _, q in plane] + [q for _, q in parts])
    weights = (wg, wu, wd)
    outs = (og, ou, od)
    todo = units(wg.shape[2])
    sends, waits, local = [], [], []
    cross, right, left, far = {}, {}, {}, {}

    def begin(u):
        w, c = todo[u]
        cross[u] = remote(
            weights[w].at[pl.ds(1 - h, 2), :, c],
            zbuf[u].at[:, h, rows16(z), :],
            ys.at[u],
            yr.at[u],
            over,
        )
        sends.append(cross[u])
        zbuf[u][:, h, rows16(z), :] = weights[w][pl.ds(h, 2), :, c]

    def ring(u, s):
        if s == 0:
            cross[u].wait_recv()
        else:
            right[u].wait_recv()
            left[u].wait_recv()
        if s == 4:
            return
        cr, cl = rows16(around(z, -s, NZ)), rows16(around(z, s, NZ))
        if s < 3:
            r, l = zbuf[u].at[:, :, cr, :], zbuf[u].at[:, :, cl, :]
        else:
            r, l = zbuf[u].at[:, 0, cr, :], zbuf[u].at[:, 1, cl, :]
        right[u] = remote(r, r, zs.at[u, 0, s], zr.at[u, 0, s], zright)
        left[u] = remote(l, l, zs.at[u, 1, s], zr.at[u, 1, s], zleft)
        sends.extend([right[u], left[u]])

    def spread(u):
        w, c = todo[u]
        out = outs[w]
        for d in (2, 1, 3, 0):
            f = flags[h * HALF + around(x, d, NX) * NZ + z]
            sbuf[u, d] = zbuf[u][f]
            if d == 2:
                a = remote(sbuf.at[u, 2, 0], relay.at[u, 0], xs.at[u, 0], xr.at[u, 0], xright)
                b = remote(sbuf.at[u, 2, 1], relay.at[u, 1], xs.at[u, 1], xr.at[u, 1], xleft)
                far[u] = (a, b)
                sends.extend([a, b])
            elif d == 0:
                a = pltpu.make_async_copy(sbuf.at[u, 0], out.at[:, x, :, c], own.at[u])
                a.start()
                local.append(a)
            else:
                i, peer = (2, xright) if d == 1 else (3, xleft)
                a = remote(sbuf.at[u, d], out.at[:, x, :, c], xs.at[u, i], xr.at[u, i], peer)
                sends.append(a)
                waits.append(a)

    def pass_on(u):
        w, c = todo[u]
        a, b = far[u]
        for i, (got, by, peer) in enumerate(((a, -1, xright), (b, 1, xleft))):
            got.wait_recv()
            a = remote(
                relay.at[u, i],
                outs[w].at[i, around(x, by, NX), :, c],
                xs.at[u, 4 + i],
                xr.at[u, 4 + i],
                peer,
            )
            sends.append(a)
            waits.append(a)

    yx = h * NX + x
    stage = {}

    def tokens_z():
        stage["z"] = []
        for d in range(1, NZ):
            to = around(z, d, NZ)
            stage["z"].append(
                remote(tok.at[:, to], tmid.at[z], ts.at[d], tr.at[d], zline[d - 1])
            )
        a = pltpu.make_async_copy(tok.at[:, z], tmid.at[z], tl.at[0])
        a.start()
        stage["zl"] = a

    def tokens_plane():
        stage["zl"].wait()
        for c in stage["z"]:
            c.wait_recv()
        sends.extend(stage["z"])
        stage["p"] = []
        to = rows.at[pl.ds(yx * NZ, NZ)]
        for d in range(1, 2 * NX):
            k, peer = plane[d - 1]
            stage["p"].append(
                remote(tmid.at[:, k], to, ts.at[NZ + d], tr.at[NZ + d], peer)
            )
        a = pltpu.make_async_copy(tmid.at[:, yx], to, tl.at[1])
        a.start()
        stage["pl"] = a

    def compact():
        stage["pl"].wait()
        for c in stage["p"]:
            c.wait_recv()
        sends.extend(stage["p"])
        groups = rows.shape[0]
        spot = lax.broadcasted_iota(jnp.int32, (groups, SLOT, 128), 1)
        head = rows[:, :, 0:128].astype(F32)
        count = jnp.sum(jnp.where(spot == CAP, head, 0.0), axis=1)
        i = lax.broadcasted_iota(jnp.int32, (groups, groups), 0)
        j = lax.broadcasted_iota(jnp.int32, (groups, groups), 1)
        lower = jnp.where(i > j, 1.0, 0.0).astype(BF)
        before = jnp.dot(lower, count.astype(BF), preferred_element_type=F32)
        spot = spot.astype(F32)
        rank = jnp.where(spot < count[:, None, :], before[:, None, :] + spot, -1.0)
        rank = rank.reshape(groups * SLOT, 128)
        lane = lax.broadcasted_iota(jnp.int32, (groups * SLOT, 128), 1)
        for b in range(close.shape[1] // 128):
            hit = rank == (lane + b * 128).astype(F32)
            close[:, b * 128 : (b + 1) * 128] = jnp.where(hit, 1.0, 0.0).astype(BF)
        feats = rows.shape[2] // 2
        for b in range(2):
            part = rows[:, :, b * feats : (b + 1) * feats].reshape(groups * SLOT, feats)
            picked = lax.dot_general(
                close[...], part, (((0,), (0,)), ((), ())), preferred_element_type=F32
            )
            mine[b] = picked.astype(BF)
        here = lanes_of(p, feats)
        stage["m"] = []
        for b, full in enumerate((fx, fdy)):
            a = pltpu.make_async_copy(mine.at[b], full.at[:, here], ml.at[b])
            a.start()
            local.append(a)
            for i in (1, 0):
                a = remote(mine.at[b], full.at[:, here], ms.at[i, b], mr.at[i, b], parts[i][1])
                sends.append(a)
                stage["m"].append(a)

    def share():
        for c in stage["m"]:
            c.wait_recv()
        there = lanes_of(parts[1][0], fx.shape[1] // 4)
        for b, full in enumerate((fx, fdy)):
            view = full.at[:, there]
            a = remote(view, view, ms.at[2, b], mr.at[2, b], parts[0][1])
            sends.append(a)
            waits.append(a)

    for u in range(n):
        begin(u)
    for t in range(2 * n + 4):
        for u in range(n):
            s = t - 2 * u
            if s == 4 and u > 0:
                pass_on(u - 1)
            if 0 <= s <= 4:
                ring(u, s)
            if s == 4:
                spread(u)
        if t == HOOKS[0]:
            tokens_z()
        elif t == HOOKS[1]:
            tokens_plane()
        elif t == HOOKS[2]:
            compact()
        elif t == HOOKS[3]:
            share()
    pass_on(n - 1)
    for c in waits:
        c.wait_recv()
    for c in sends:
        c.wait_send()
    for c in local:
        c.wait()


def gather_all(flags, wg, wu, wd, tok, rows, feats):
    cols = wg.shape[2]
    n = 3 * SPLIT
    wide = cols // SPLIT
    vm = pl.BlockSpec(memory_space=pltpu.VMEM)
    hbm = pl.BlockSpec(memory_space=pl.ANY)
    dma = pltpu.SemaphoreType.DMA
    out = jax.ShapeDtypeStruct((2, NX, 16 * NZ, cols), BF)
    full = jax.ShapeDtypeStruct((rows, 4 * feats), BF)
    close = jax.ShapeDtypeStruct((2 * HALF * SLOT, rows), BF)
    return pl.pallas_call(
        gather_kernel,
        out_shape=(out, out, out, full, full, close),
        in_specs=[pl.BlockSpec(memory_space=pltpu.SMEM), vm, vm, vm, vm],
        out_specs=[hbm] * 5 + [vm],
        scratch_shapes=[pltpu.VMEM((2, 2, 16 * NZ, wide), BF)] * n
        + [
            pltpu.VMEM((n, 4, 2, 16 * NZ, wide), BF),
            pltpu.VMEM((n, 2, 16 * NZ, wide), BF),
            pltpu.VMEM((NZ, 2 * NX, SLOT, 2 * feats), BF),
            pltpu.VMEM((2 * HALF, SLOT, 2 * feats), BF),
            pltpu.VMEM((2, rows, feats), BF),
            dma((n,)),
            dma((n,)),
            dma((n, 2, 4)),
            dma((n, 2, 4)),
            dma((n, 6)),
            dma((n, 6)),
            dma((n,)),
            dma((16,)),
            dma((16,)),
            dma((2,)),
            dma((3, 2)),
            dma((3, 2)),
            dma((2,)),
        ],
        compiler_params=pltpu.CompilerParams(
            collective_id=0, has_side_effects=True, vmem_limit_bytes=48 * 1024 * 1024
        ),
        cost_estimate=pl.CostEstimate(flops=0, bytes_accessed=200_000_000, transcendentals=0),
        name="gather_all",
    )(flags, wg, wu, wd, tok.reshape(2 * NX, NZ, SLOT, 2 * feats))


def reduce_kernel(flags, gg, gu, gd, res, dx, close, og, ou, od, back, *scratch):
    n = 3 * SPLIT
    rbuf, relay, zsum, zin, keep, ysend, yin, pin, spread_rows, tmid = scratch[:10]
    ys, yr, zs, zr, xs, xr, own, ts, tr, tl, ms, mr, ml = scratch[10:]
    p, h, x, z = place()
    at, zline, plane, parts = peers_of(p, h, x, z)
    over = at(1 - h, x, z)
    zright, zleft = at(h, x, around(z, 1, NZ)), at(h, x, around(z, -1, NZ))
    xr1, xl1 = around(x, 1, NX), around(x, -1, NX)
    xright, xleft = at(h, xr1, z), at(h, xl1, z)
    greet(zline + [q for _, q in plane] + [q for _, q in parts])
    grads = (gg, gu, gd)
    outs = (og, ou, od)
    todo = units(gg.shape[3])
    sends = []
    first, steps, cross, stage = {}, {}, {}, {}

    def spread(u):
        w, c = todo[u]
        g = grads[w]
        x2 = around(x, 2, NX)
        a = remote(g.at[0, x2, :, c], relay.at[u, 0], xs.at[u, 0], xr.at[u, 0], xright)
        b = remote(g.at[1, x2, :, c], relay.at[u, 1], xs.at[u, 1], xr.at[u, 1], xleft)
        i = remote(g.at[:, xr1, :, c], rbuf.at[u, 1], xs.at[u, 2], xr.at[u, 2], xright)
        j = remote(g.at[:, xl1, :, c], rbuf.at[u, 3], xs.at[u, 3], xr.at[u, 3], xleft)
        e = pltpu.make_async_copy(g.at[:, x, :, c], rbuf.at[u, 0], own.at[u])
        e.start()
        sends.extend([a, b, i, j])
        first[u] = (a, b, i, j, e)

    def pass_on(u):
        a, b, i, j, e = first[u]
        a.wait_recv()
        r = remote(relay.at[u, 0], rbuf.at[u, 2, 0], xs.at[u, 4], xr.at[u, 4], xright)
        b.wait_recv()
        l = remote(relay.at[u, 1], rbuf.at[u, 2, 1], xs.at[u, 5], xr.at[u, 5], xleft)
        sends.extend([r, l])
        first[u] = (i, j, r, l, e)

    marks = [flags[h * HALF + around(x, by, NX) * NZ + z].astype(F32) for by in (0, -1, 2, 1)]

    def bins(u):
        i, j, r, l, e = first[u]
        e.wait()
        for c in (i, j, r, l):
            c.wait_recv()

        def body(i, _):
            y = lax.div(i, NZ)
            at_rows = rows16(lax.rem(i, NZ))
            low = high = None
            for k in range(4):
                v = rbuf[u, k, y, at_rows, :].astype(F32)
                b = v * marks[k]
                a = v - b
                low = a if low is None else low + a
                high = b if high is None else high + b
            zsum[u, 0, y, at_rows, :] = low.astype(BF)
            zsum[u, 1, y, at_rows, :] = high.astype(BF)
            return 0

        lax.fori_loop(0, 2 * NZ, body, 0)

    def plus(a, b):
        return (a.astype(F32) + b.astype(F32)).astype(BF)

    def ring(u, s):
        for way, (peer, sign) in enumerate(((zright, 1), (zleft, -1))):
            part = rows16(around(z, sign * (4 - s), NZ))
            if s == 0:
                c = remote(
                    zsum.at[u, :, way, part, :],
                    zin.at[u, way, 0, :, way],
                    zs.at[u, way, 0],
                    zr.at[u, way, 0],
                    peer,
                )
            else:
                steps[u, way].wait_recv()
                if s == 1:
                    zin[u, way, 0, :, way] = plus(
                        zin[u, way, 0, :, way], zsum[u, :, way, part, :]
                    )
                    zin[u, way, 0, :, 1 - way] = zsum[u, :, 1 - way, part, :]
                else:
                    zin[u, way, s - 1] = plus(zin[u, way, s - 1], zsum[u, :, :, part, :])
                c = remote(
                    zin.at[u, way, s - 1],
                    zin.at[u, way, s],
                    zs.at[u, way, s],
                    zr.at[u, way, s],
                    peer,
                )
            steps[u, way] = c
            sends.append(c)

    def total(u, y):
        part = rows16(z)
        v = zsum[u, :, y, part, :].astype(F32)
        v = v + zin[u, 0, 3, :, y].astype(F32)
        return v + zin[u, 1, 3, :, y].astype(F32)

    def swap(u):
        steps[u, 0].wait_recv()
        steps[u, 1].wait_recv()
        ysend[u] = total(u, 1 - h).astype(BF)
        cross[u] = remote(ysend.at[u], yin.at[u], ys.at[u], yr.at[u], over)
        sends.append(cross[u])
        keep[u] = total(u, h)

    def finish(u):
        w, c = todo[u]
        cross[u].wait_recv()
        out = outs[w]
        out[2 * h, :, c] = keep[u, h]
        out[1, :, c] = keep[u, 1 - h] + yin[u, h].astype(F32)
        out[2 - 2 * h, :, c] = yin[u, 1 - h].astype(F32)

    yx = h * NX + x
    feats = res.shape[1] // 4

    def sums_out():
        stage["m"] = []
        for i in (1, 2, 0):
            q, peer = parts[i]
            for b, v in enumerate((res, dx)):
                stage["m"].append(
                    remote(v.at[:, lanes_of(q, feats)], pin.at[i, b], ms.at[i, b], mr.at[i, b], peer)
                )
        here = lanes_of(p, feats)
        stage["ml"] = []
        for b, v in enumerate((res, dx)):
            a = pltpu.make_async_copy(v.at[:, here], pin.at[3, b], ml.at[b])
            a.start()
            stage["ml"].append(a)

    def widen():
        for c in stage["ml"]:
            c.wait()
        for c in stage["m"]:
            c.wait_recv()
        sends.extend(stage["m"])
        groups = spread_rows.shape[0]
        for b in range(2):
            v = pin[3, b].astype(F32)
            for i in range(3):
                v = v + pin[i, b].astype(F32)
            v = jnp.dot(close[...], v.astype(BF), preferred_element_type=F32).astype(BF)
            spread_rows[:, :, b * feats : (b + 1) * feats] = v.reshape(groups, SLOT, feats)
        stage["p"] = []
        for d in range(1, 2 * NX):
            k, peer = plane[d - 1]
            stage["p"].append(
                remote(
                    spread_rows.at[pl.ds(k * NZ, NZ)],
                    tmid.at[:, yx],
                    ts.at[NZ + d],
                    tr.at[NZ + d],
                    peer,
                )
            )
        a = pltpu.make_async_copy(spread_rows.at[pl.ds(yx * NZ, NZ)], tmid.at[:, yx], tl.at[0])
        a.start()
        stage["pl"] = a

    def homeward():
        stage["pl"].wait()
        for c in stage["p"]:
            c.wait_recv()
        sends.extend(stage["p"])
        stage["z"] = []
        for d in range(1, NZ):
            to = around(z, d, NZ)
            stage["z"].append(
                remote(tmid.at[to], back.at[:, z], ts.at[d], tr.at[d], zline[d - 1])
            )
        a = pltpu.make_async_copy(tmid.at[z], back.at[:, z], tl.at[1])
        a.start()
        stage["zl"] = a

    spread(0)
    sums_out()
    spread(1)
    pass_on(0)
    for u in range(n):
        if u + 2 < n:
            spread(u + 2)
        if u + 1 < n:
            pass_on(u + 1)
        bins(u)
        ring(u, 0)
        if u > 0:
            ring(u - 1, 2)
        ring(u, 1)
        if u > 0:
            ring(u - 1, 3)
            swap(u - 1)
        if u == HOOKS[4]:
            widen()
        if u == HOOKS[5]:
            homeward()
    ring(n - 1, 2)
    ring(n - 1, 3)
    swap(n - 1)
    for u in range(n):
        finish(u)
    stage["zl"].wait()
    for c in stage["z"]:
        c.wait_recv()
        c.wait_send()
    for c in sends:
        c.wait_send()


def reduce_all(flags, gg, gu, gd, res, dx, close):
    cols = gg.shape[1]
    rows = res.shape[0]
    feats = res.shape[1] // 4
    n = 3 * SPLIT
    wide = cols // SPLIT
    shape = (2, NX, 16 * NZ, cols)
    vm = pl.BlockSpec(memory_space=pltpu.VMEM)
    hbm = pl.BlockSpec(memory_space=pl.ANY)
    dma = pltpu.SemaphoreType.DMA
    out = jax.ShapeDtypeStruct((3, 16, cols), F32)
    back = jax.ShapeDtypeStruct((2 * NX, NZ, SLOT, 2 * feats), BF)
    return pl.pallas_call(
        reduce_kernel,
        out_shape=(out, out, out, back),
        in_specs=[pl.BlockSpec(memory_space=pltpu.SMEM)] + [hbm] * 5 + [vm],
        out_specs=[vm] * 3 + [hbm],
        scratch_shapes=[
            pltpu.VMEM((n, 4, 2, 16 * NZ, wide), BF),
            pltpu.VMEM((n, 2, 16 * NZ, wide), BF),
            pltpu.VMEM((n, 2, 2, 16 * NZ, wide), BF),
            pltpu.VMEM((n, 2, 4, 2, 2, 16, wide), BF),
            pltpu.VMEM((n, 2, 16, wide), F32),
            pltpu.VMEM((n, 2, 16, wide), BF),
            pltpu.VMEM((n, 2, 16, wide), BF),
            pltpu.VMEM((4, 2, rows, feats), BF),
            pltpu.VMEM((2 * HALF, SLOT, 2 * feats), BF),
            pltpu.VMEM((NZ, 2 * NX, SLOT, 2 * feats), BF),
            dma((n,)),
            dma((n,)),
            dma((n, 2, 4)),
            dma((n, 2, 4)),
            dma((n, 6)),
            dma((n, 6)),
            dma((n,)),
            dma((16,)),
            dma((16,)),
            dma((2,)),
            dma((3, 2)),
            dma((3, 2)),
            dma((2,)),
        ],
        compiler_params=pltpu.CompilerParams(
            collective_id=1, has_side_effects=True, vmem_limit_bytes=48 * 1024 * 1024
        ),
        cost_estimate=pl.CostEstimate(flops=0, bytes_accessed=200_000_000, transcendentals=0),
        name="reduce_all",
    )(flags, gg.reshape(shape), gu.reshape(shape), gd.reshape(shape), res, dx, close)


def project_rows(x, dy, wg, wu, wd):
    gate = jnp.dot(x, wg, preferred_element_type=F32)
    up = jnp.dot(x, wu, preferred_element_type=F32)
    sig = jax.nn.sigmoid(gate)
    silu = gate * sig
    hidden = (silu * up).astype(BF)
    out = lax.dot_general(hidden, wd, (((1,), (1,)), ((), ())), preferred_element_type=F32)
    dhidden = jnp.dot(dy, wd, preferred_element_type=F32)
    dgate = (dhidden * up * sig * (1.0 + gate * (1.0 - sig))).astype(BF)
    dup = (dhidden * silu).astype(BF)
    dx = lax.dot_general(dgate, wg, (((1,), (1,)), ((), ())), preferred_element_type=F32)
    dx = dx + lax.dot_general(dup, wu, (((1,), (1,)), ((), ())), preferred_element_type=F32)
    over_rows = (((0,), (0,)), ((), ()))
    grad_g = lax.dot_general(x, dgate, over_rows, preferred_element_type=F32).astype(BF)
    grad_u = lax.dot_general(x, dup, over_rows, preferred_element_type=F32).astype(BF)
    grad_d = lax.dot_general(dy, hidden, over_rows, preferred_element_type=F32).astype(BF)
    return out, dx, grad_g, grad_u, grad_d


def shards(tokens, cotangent, tags, counts, target, gate_weight, up_weight, down_weight):
    groups = lax.axis_size("group")
    rows, feats = tokens.shape
    total = rows * groups
    start_b = groups * counts[0] // total
    start_c = groups * (counts[0] + counts[1]) // total
    devices = jnp.arange(groups, dtype=jnp.int32)
    device_mod = (devices >= start_b).astype(jnp.int32) + (devices >= start_c).astype(jnp.int32)
    flags = device_mod - devices // HALF
    base = jnp.where(tags == 0, 0, jnp.where(tags == 1, start_b, start_c))
    dest = base + target
    onehot = (dest[:, None] == devices[None, :]).astype(BF)
    places = jnp.arange(rows, dtype=jnp.int32)
    lower = (places[:, None] > places[None, :]).astype(BF)
    earlier = jnp.dot(lower, onehot, preferred_element_type=F32)
    slot = jnp.sum(earlier * onehot.astype(F32), axis=1).astype(jnp.int32)
    sent = jnp.sum(onehot.astype(F32), axis=0)
    position = dest * SLOT + slot
    wide = groups * SLOT
    lanes = jnp.arange(wide, dtype=jnp.int32)
    both = jnp.concatenate([tokens, cotangent], axis=1)
    into = (lanes[:, None] == position[None, :]).astype(BF)
    send = jnp.dot(into, both, preferred_element_type=F32).reshape(groups, SLOT, 2 * feats)
    tail = (jnp.arange(SLOT, dtype=jnp.int32) >= CAP)[None, :, None]
    send = jnp.where(tail, sent[:, None, None], send).astype(BF).reshape(wide, 2 * feats)
    w_gate, w_up, w_down, full_x, full_dy, close = gather_all(
        flags, gate_weight, up_weight, down_weight, send, rows, feats
    )
    depth = full_x.shape[1]
    w_gate, w_up, w_down = (w.reshape(depth, -1) for w in (w_gate, w_up, w_down))
    out, dx, grad_g, grad_u, grad_d = project_rows(full_x, full_dy, w_gate, w_up, w_down)
    gate_grad, up_grad, down_grad, back = reduce_all(
        flags, grad_g, grad_u, grad_d, out.astype(BF), dx.astype(BF), close
    )
    out_of = (position[:, None] == lanes[None, :]).astype(BF)
    result = jnp.dot(out_of, back.reshape(wide, 2 * feats), preferred_element_type=F32).astype(BF)
    return result[:, :feats], result[:, feats:], gate_grad, up_grad, down_grad


def solution(mesh):
    in_specs = (
        P("group", "mp"),
        P("group", "mp"),
        P("group"),
        P(),
        P("group"),
        P(None, "group", "mp"),
        P(None, "group", "mp"),
        P(None, "group", "mp"),
    )
    out_specs = (
        P("group", "mp"),
        P("group", "mp"),
        P(None, "group", "mp"),
        P(None, "group", "mp"),
        P(None, "group", "mp"),
    )
    return jax.shard_map(shards, mesh=mesh, in_specs=in_specs, out_specs=out_specs, check_vma=False)
```

time: 597 us -> 287 us (0.48)
  waiting for transfers between devices: 280 us -> 0 us
  Pallas kernels: 0 us -> 256 us
  blocking collectives: 168 us -> 0 us
  starting transfers between devices: 59.5 us -> 0 us
  matrix products: 38.1 us -> 17.3 us
  local copies, waits for them, and re-layouts: 21.4 us -> 6.17 us
  between operations: 16.4 us -> 2.78 us
  other arithmetic: 11.3 us -> 0.98 us
    pallas_call x0 -> x2, Pallas kernels: none -> 256 us  [the longest x1 129 us: reduce_all(): pl.pallas_call(reduce_kernel, out_shape=(out, out, out, back), in_specs=[...]
    all_to_all x9 -> x0, waiting for transfers between devices: 255 us -> none  [the longest x1 48.4 us: shards(): lax.all_to_all(pick_g, 'group', split_axis=0, concat_axis=0, tiled=True)]
    psum x1 -> x0, blocking collectives: 113 us -> none  [shards(): out_sum, dx_sum = lax.psum((out_part, dx_part), 'mp')]
    all_to_all x9 -> x0, starting transfers between devices: 59.2 us -> none  [the longest x1 12.7 us: shards(): lax.all_to_all(send_x, 'group', split_axis=0, concat_axis=0, tiled=True)]
    all_to_all x1 -> x0, blocking collectives: 54.8 us -> none  [shards(): lax.all_to_all(pick_u, 'group', split_axis=0, concat_axis=0, tiled=True)]
    all_gather x2 -> x0, waiting for transfers between devices: 25 us -> none  [the longest x1 25 us: shards(): lax.all_gather(recv_dy, 'mp', axis=1, tiled=True)]
    dot_general x7 -> x9, matrix products: 29.4 us -> 14.2 us  [the longest x1 2.62 us: project_rows(): lax.dot_general(x, dup, over_rows, preferred_element_type=F32).astype(BF)]
  transfers between devices with their start and end apart: 11 -> 0, of which waited for: 10 -> 0; matrix products, arithmetic and copies ran while one was open for 6% -> 0% of each run, Pallas kernels for 0% -> 0%
where the time goes in v2:
time: 287 us; the launch traced here: 283 us
  Pallas kernels  256 us (89%)
  matrix products  17.3 us (6%)
  local copies, waits for them, and re-layouts  6.17 us (2%)
    pallas_call x1, Pallas kernels, reduce_all(): pl.pallas_call(reduce_kernel, out_shape=(out, out, out, back), in_specs=[...  129 us
    pallas_call x1, Pallas kernels, gather_all(): pl.pallas_call(gather_kernel, out_shape=(out, out, out, full, full, close...  127 us

profile of v2, /device:TPU:16, one launch (start us, length us, event | category | flops | bytes accessed | tf_op | source)
XLA Modules:
  0.0 282.9 jit_solution(2962040758745846872)
XLA Ops:
  0.6 1.3 fusion.16
  4.0 0.7 select_add_fusion
  4.7 0.1 convert_reduce_fusion
  4.8 0.1 broadcast_in_dim.41
  4.9 0.2 fusion.4
  5.1 1.7 fusion.2
  6.9 0.0 copy-start
  6.9 0.0 copy-start.1
  6.9 0.0 copy-start.2
  6.9 0.1 select_convert_fusion.tok
  7.0 0.7 copy-done
  7.8 0.0 copy-done.1
  7.8 0.0 copy-done.2
  7.9 126.7 %gather_all.1 = (bf16[2,4,128,1024]{3,2,1,0:T(8,128)(2,1)S(1)}, bf16[2,4,128,1024]{3,2,1,0:T(8,128)(2,1)}, bf16[2,4,128,1024]{3,2,1,0:T(8,128)(2,1)}, bf16[384,1...) custom-call(s32[64]{0:T(128)S(1)} %fusion.12.flags, ...), custom_call_target="tpu_custom_call" | custom-call | bytes 200000000 | tf_op jit(solution)/shard_map/gather_all/pallas_call | solution.py:280
  134.5 2.6 fusion.17
  137.1 0.0 copy-start.4
  137.1 1.0 fusion.18
  138.1 0.6 copy-done.4
  138.7 1.5 multiply_convert_fusion
  140.2 1.0 fusion.19
  141.3 0.0 copy-start.3
  141.3 1.0 add_convert_fusion.dx
  142.3 0.6 copy-done.3
  142.9 1.0 convolution_convert_fusion.3.res
  143.9 2.6 convolution_convert_fusion
  146.5 1.3 convolution_convert_fusion.2
  147.8 2.6 convolution_convert_fusion.1
  150.5 129.0 %reduce_all.1 = (f32[3,16,1024]{2,1,0:T(8,128)S(1)}, f32[3,16,1024]{2,1,0:T(8,128)S(1)}, f32[3,16,1024]{2,1,0:T(8,128)S(1)}, bf16[8,8,16,512]{3,2,1,0:T(8,128)(2,1)S(1)}) custom-call(s32[64]{0:T(128)S(1)} %fusion.12.flags, bf16[2,4,128,1024]{3,2,1,0:T(8,128)(2,1)S(1)} %bitcast.31, bf16[2,4,128,1024]{3,2,1,0:T(8,128)(2,1)} %bitcast.36, ...), custom_call_target="tpu_custom_call" | custom-call | bytes 200000000 | tf_op jit(solution)/shard_map/reduce_all/pallas_call | solution.py:540
  279.5 0.6 fusion.3
  280.1 0.8 fusion.15
  280.9 0.7 copy.16
  281.6 0.7 copy.17
  282.2 0.7 copy.18
  (3 shorter events, 0.0 us)
Async XLA Ops:
  6.9 0.9 copy-start
  6.9 0.9 copy-start.1
  6.9 1.0 copy-start.2
  137.1 1.6 copy-start.4
  141.3 1.6 copy-start.3

commit v3 on v2

--- a/solution.py
+++ b/solution.py
@@ -11,8 +11,15 @@
 HALF = NX * NZ
 CAP = 12
 SLOT = 16
-SPLIT = 2
-HOOKS = (1, 6, 9, 12, 1, 3)
+UNITS = (
+    (0, 0, 256),
+    (0, 256, 384),
+    (0, 640, 384),
+    (1, 0, 512),
+    (1, 512, 512),
+    (2, 0, 640),
+)
+FLIP = (2, 640, 384)
 
 
 def place():
@@ -50,11 +57,6 @@
     )
     copy.start()
     return copy
-
-
-def units(cols):
-    wide = cols // SPLIT
-    return [(w, pl.ds(i * wide, wide)) for w in range(3) for i in range(SPLIT)]
 
 
 def peers_of(p, h, x, z):
@@ -80,86 +82,94 @@
 
 
 def gather_kernel(flags, wg, wu, wd, tok, og, ou, od, fx, fdy, close, *scratch):
-    n = 3 * SPLIT
-    zbuf = scratch[:n]
-    sbuf, relay, tmid, rows, mine = scratch[n : n + 5]
-    ys, yr, zs, zr, xs, xr, own, ts, tr, tl, ms, mr, ml = scratch[n + 5 :]
+    n = len(UNITS)
+    zbuf, sbuf = scratch[:n], scratch[n : 2 * n]
+    fbuf, fsend, tmid, rows, mine = scratch[2 * n : 2 * n + 5]
+    ys, yr, zs, zr, xs, xr, own, fs, fr, gs, gr, ts, tr, tl, ms, mr, ml = scratch[2 * n + 5 :]
     p, h, x, z = place()
     at, zline, plane, parts = peers_of(p, h, x, z)
     over = at(1 - h, x, z)
-    zright, zleft = at(h, x, around(z, 1, NZ)), at(h, x, around(z, -1, NZ))
-    xright, xleft = at(h, around(x, 1, NX), z), at(h, around(x, -1, NX), z)
+    xline = [at(h, around(x, d, NX), z) for d in range(1, NX)]
     greet(zline + [q for _, q in plane] + [q for _, q in parts])
     weights = (wg, wu, wd)
     outs = (og, ou, od)
-    todo = units(wg.shape[2])
     sends, waits, local = [], [], []
-    cross, right, left, far = {}, {}, {}, {}
+    cross, near, later = {}, {}, {}
 
     def begin(u):
-        w, c = todo[u]
+        w, c0, width = UNITS[u] if u < n else FLIP
+        c = pl.ds(c0, width)
+        if u < n:
+            theirs = zbuf[u].at[:, h, rows16(z), :]
+        else:
+            theirs = fbuf.at[:, h, x]
         cross[u] = remote(
-            weights[w].at[pl.ds(1 - h, 2), :, c],
-            zbuf[u].at[:, h, rows16(z), :],
-            ys.at[u],
-            yr.at[u],
-            over,
+            weights[w].at[pl.ds(1 - h, 2), :, c], theirs, ys.at[u], yr.at[u], over
         )
         sends.append(cross[u])
-        zbuf[u][:, h, rows16(z), :] = weights[w][pl.ds(h, 2), :, c]
-
-    def ring(u, s):
-        if s == 0:
-            cross[u].wait_recv()
-        else:
-            right[u].wait_recv()
-            left[u].wait_recv()
-        if s == 4:
-            return
-        cr, cl = rows16(around(z, -s, NZ)), rows16(around(z, s, NZ))
-        if s < 3:
-            r, l = zbuf[u].at[:, :, cr, :], zbuf[u].at[:, :, cl, :]
-        else:
-            r, l = zbuf[u].at[:, 0, cr, :], zbuf[u].at[:, 1, cl, :]
-        right[u] = remote(r, r, zs.at[u, 0, s], zr.at[u, 0, s], zright)
-        left[u] = remote(l, l, zs.at[u, 1, s], zr.at[u, 1, s], zleft)
-        sends.extend([right[u], left[u]])
+        theirs[...] = weights[w][pl.ds(h, 2), :, c]
+
+    def first(u):
+        cross[u].wait_recv()
+        v = zbuf[u].at[:, :, rows16(z), :]
+        near[u] = [
+            remote(v, v, zs.at[u, i], zr.at[u, i], zline[d % NZ - 1])
+            for i, d in ((2, 2), (3, -2), (0, 1), (1, -1))
+        ]
+        sends.extend(near[u])
+
+    def second(u):
+        ahead, behind = near[u][:2]
+        later[u] = near[u][2:]
+        for i, (got, by) in enumerate(((ahead, 1), (behind, -1))):
+            got.wait_recv()
+            chunk = rows16(around(z, -2 * by, NZ))
+            v = zbuf[u].at[:, :, chunk, :]
+            a = remote(v, v, zs.at[u, 4 + i], zr.at[u, 4 + i], zline[by % NZ - 1])
+            v = zbuf[u].at[:, i, chunk, :]
+            b = remote(v, v, zs.at[u, 6 + i], zr.at[u, 6 + i], zline[2 * by % NZ - 1])
+            later[u].extend([a, b])
+            sends.extend([a, b])
 
     def spread(u):
-        w, c = todo[u]
-        out = outs[w]
+        for c in later[u]:
+            c.wait_recv()
+        w, c0, width = UNITS[u]
+        out = outs[w].at[:, x, :, pl.ds(c0, width)]
         for d in (2, 1, 3, 0):
             f = flags[h * HALF + around(x, d, NX) * NZ + z]
-            sbuf[u, d] = zbuf[u][f]
-            if d == 2:
-                a = remote(sbuf.at[u, 2, 0], relay.at[u, 0], xs.at[u, 0], xr.at[u, 0], xright)
-                b = remote(sbuf.at[u, 2, 1], relay.at[u, 1], xs.at[u, 1], xr.at[u, 1], xleft)
-                far[u] = (a, b)
-                sends.extend([a, b])
-            elif d == 0:
-                a = pltpu.make_async_copy(sbuf.at[u, 0], out.at[:, x, :, c], own.at[u])
+            sbuf[u][d] = zbuf[u][f]
+            if d == 0:
+                a = pltpu.make_async_copy(sbuf[u].at[0], out, own.at[u])
                 a.start()
                 local.append(a)
             else:
-                i, peer = (2, xright) if d == 1 else (3, xleft)
-                a = remote(sbuf.at[u, d], out.at[:, x, :, c], xs.at[u, i], xr.at[u, i], peer)
+                a = remote(sbuf[u].at[d], out, xs.at[u, d], xr.at[u, d], xline[d - 1])
                 sends.append(a)
                 waits.append(a)
 
-    def pass_on(u):
-        w, c = todo[u]
-        a, b = far[u]
-        for i, (got, by, peer) in enumerate(((a, -1, xright), (b, 1, xleft))):
-            got.wait_recv()
-            a = remote(
-                relay.at[u, i],
-                outs[w].at[i, around(x, by, NX), :, c],
-                xs.at[u, 4 + i],
-                xr.at[u, 4 + i],
-                peer,
-            )
-            sends.append(a)
-            waits.append(a)
+    def flip_first():
+        cross[n].wait_recv()
+        v = fbuf.at[:, :, x]
+        near[n] = [remote(v, v, fs.at[d], fr.at[d], xline[d - 1]) for d in (2, 1, 3)]
+        sends.extend(near[n])
+
+    def flip_second():
+        for c in near[n]:
+            c.wait_recv()
+        w, c0, width = FLIP
+        out = outs[w].at[:, :, rows16(z), pl.ds(c0, width)]
+        for d in (4, 3, 5, 2, 6, 1, 7, 0):
+            f = flags[h * HALF + x * NZ + around(z, d, NZ)]
+            fsend[d] = fbuf[f]
+            if d == 0:
+                a = pltpu.make_async_copy(fsend.at[0], out, own.at[n])
+                a.start()
+                local.append(a)
+            else:
+                a = remote(fsend.at[d], out, gs.at[d], gr.at[d], zline[d - 1])
+                sends.append(a)
+                waits.append(a)
 
     yx = h * NX + x
     stage = {}
@@ -239,26 +249,32 @@
             sends.append(a)
             waits.append(a)
 
-    for u in range(n):
+    for u in range(n + 1):
         begin(u)
-    for t in range(2 * n + 4):
-        for u in range(n):
-            s = t - 2 * u
-            if s == 4 and u > 0:
-                pass_on(u - 1)
-            if 0 <= s <= 4:
-                ring(u, s)
-            if s == 4:
-                spread(u)
-        if t == HOOKS[0]:
-            tokens_z()
-        elif t == HOOKS[1]:
-            tokens_plane()
-        elif t == HOOKS[2]:
-            compact()
-        elif t == HOOKS[3]:
-            share()
-    pass_on(n - 1)
+    first(0)
+    flip_first()
+    second(0)
+    first(1)
+    tokens_z()
+    spread(0)
+    second(1)
+    first(2)
+    spread(1)
+    second(2)
+    flip_second()
+    first(3)
+    spread(2)
+    tokens_plane()
+    second(3)
+    first(4)
+    spread(3)
+    second(4)
+    first(5)
+    compact()
+    spread(4)
+    second(5)
+    share()
+    spread(5)
     for c in waits:
         c.wait_recv()
     for c in sends:
@@ -269,8 +285,7 @@
 
 def gather_all(flags, wg, wu, wd, tok, rows, feats):
     cols = wg.shape[2]
-    n = 3 * SPLIT
-    wide = cols // SPLIT
+    n = len(UNITS)
     vm = pl.BlockSpec(memory_space=pltpu.VMEM)
     hbm = pl.BlockSpec(memory_space=pl.ANY)
     dma = pltpu.SemaphoreType.DMA
@@ -282,20 +297,25 @@
         out_shape=(out, out, out, full, full, close),
         in_specs=[pl.BlockSpec(memory_space=pltpu.SMEM), vm, vm, vm, vm],
         out_specs=[hbm] * 5 + [vm],
-        scratch_shapes=[pltpu.VMEM((2, 2, 16 * NZ, wide), BF)] * n
+        scratch_shapes=[pltpu.VMEM((2, 2, 16 * NZ, u[2]), BF) for u in UNITS]
+        + [pltpu.VMEM((4, 2, 16 * NZ, u[2]), BF) for u in UNITS]
         + [
-            pltpu.VMEM((n, 4, 2, 16 * NZ, wide), BF),
-            pltpu.VMEM((n, 2, 16 * NZ, wide), BF),
+            pltpu.VMEM((2, 2, NX, 16, FLIP[2]), BF),
+            pltpu.VMEM((NZ, 2, NX, 16, FLIP[2]), BF),
             pltpu.VMEM((NZ, 2 * NX, SLOT, 2 * feats), BF),
             pltpu.VMEM((2 * HALF, SLOT, 2 * feats), BF),
             pltpu.VMEM((2, rows, feats), BF),
-            dma((n,)),
-            dma((n,)),
-            dma((n, 2, 4)),
-            dma((n, 2, 4)),
-            dma((n, 6)),
-            dma((n, 6)),
-            dma((n,)),
+            dma((n + 1,)),
+            dma((n + 1,)),
+            dma((n, 8)),
+            dma((n, 8)),
+            dma((n, 4)),
+            dma((n, 4)),
+            dma((n + 1,)),
+            dma((4,)),
+            dma((4,)),
+            dma((8,)),
+            dma((8,)),
             dma((16,)),
             dma((16,)),
             dma((2,)),
@@ -312,122 +332,197 @@
 
 
 def reduce_kernel(flags, gg, gu, gd, res, dx, close, og, ou, od, back, *scratch):
-    n = 3 * SPLIT
-    rbuf, relay, zsum, zin, keep, ysend, yin, pin, spread_rows, tmid = scratch[:10]
-    ys, yr, zs, zr, xs, xr, own, ts, tr, tl, ms, mr, ml = scratch[10:]
+    n = len(UNITS)
+    per = 10
+    bufs = [scratch[per * u : per * u + per] for u in range(n)]
+    ends = [b[7:] for b in bufs] + [scratch[per * n + 3 : per * n + 6]]
+    fin, fsum, fgot = scratch[per * n : per * n + 3]
+    pin, spread_rows, tmid = scratch[per * n + 6 : per * n + 9]
+    ys, yr, zs, zr, xs, xr, own, fs, fr, gs, gr, ts, tr, tl, ms, mr, ml = scratch[per * n + 9 :]
     p, h, x, z = place()
     at, zline, plane, parts = peers_of(p, h, x, z)
     over = at(1 - h, x, z)
-    zright, zleft = at(h, x, around(z, 1, NZ)), at(h, x, around(z, -1, NZ))
-    xr1, xl1 = around(x, 1, NX), around(x, -1, NX)
-    xright, xleft = at(h, xr1, z), at(h, xl1, z)
+    xline = [at(h, around(x, d, NX), z) for d in range(1, NX)]
     greet(zline + [q for _, q in plane] + [q for _, q in parts])
     grads = (gg, gu, gd)
     outs = (og, ou, od)
-    todo = units(gg.shape[3])
+    order = UNITS[::-1]
     sends = []
-    first, steps, cross, stage = {}, {}, {}, {}
+    arriving, stepping, cross, stage = {}, {}, {}, {}
 
     def spread(u):
-        w, c = todo[u]
-        g = grads[w]
-        x2 = around(x, 2, NX)
-        a = remote(g.at[0, x2, :, c], relay.at[u, 0], xs.at[u, 0], xr.at[u, 0], xright)
-        b = remote(g.at[1, x2, :, c], relay.at[u, 1], xs.at[u, 1], xr.at[u, 1], xleft)
-        i = remote(g.at[:, xr1, :, c], rbuf.at[u, 1], xs.at[u, 2], xr.at[u, 2], xright)
-        j = remote(g.at[:, xl1, :, c], rbuf.at[u, 3], xs.at[u, 3], xr.at[u, 3], xleft)
-        e = pltpu.make_async_copy(g.at[:, x, :, c], rbuf.at[u, 0], own.at[u])
-        e.start()
-        sends.extend([a, b, i, j])
-        first[u] = (a, b, i, j, e)
-
-    def pass_on(u):
-        a, b, i, j, e = first[u]
-        a.wait_recv()
-        r = remote(relay.at[u, 0], rbuf.at[u, 2, 0], xs.at[u, 4], xr.at[u, 4], xright)
-        b.wait_recv()
-        l = remote(relay.at[u, 1], rbuf.at[u, 2, 1], xs.at[u, 5], xr.at[u, 5], xleft)
-        sends.extend([r, l])
-        first[u] = (i, j, r, l, e)
-
-    marks = [flags[h * HALF + around(x, by, NX) * NZ + z].astype(F32) for by in (0, -1, 2, 1)]
+        w, c0, width = order[u]
+        g, c = grads[w], pl.ds(c0, width)
+        rbuf = bufs[u][0]
+        arriving[u] = []
+        for d in (2, 1, 3):
+            a = remote(
+                g.at[:, around(x, d, NX), :, c],
+                rbuf.at[d],
+                xs.at[u, d],
+                xr.at[u, d],
+                xline[d - 1],
+            )
+            arriving[u].append(a)
+            sends.append(a)
+        a = pltpu.make_async_copy(g.at[:, x, :, c], rbuf.at[0], own.at[u])
+        a.start()
+        arriving[u].append(a)
+
+    def arrive(u):
+        for c in arriving[u][:3]:
+            c.wait_recv()
+        arriving[u][3].wait()
+
+    def binned(terms, marks):
+        low = high = None
+        for v, m in zip(terms, marks):
+            v = v.astype(F32)
+            b = v * m
+            a = v - b
+            low = a if low is None else low + a
+            high = b if high is None else high + b
+        return low.astype(BF), high.astype(BF)
+
+    xmarks = [
+        flags[h * HALF + around(x, -d, NX) * NZ + z].astype(F32) for d in range(NX)
+    ]
 
     def bins(u):
-        i, j, r, l, e = first[u]
-        e.wait()
-        for c in (i, j, r, l):
-            c.wait_recv()
+        rbuf, zsum = bufs[u][:2]
 
         def body(i, _):
             y = lax.div(i, NZ)
-            at_rows = rows16(lax.rem(i, NZ))
-            low = high = None
-            for k in range(4):
-                v = rbuf[u, k, y, at_rows, :].astype(F32)
-                b = v * marks[k]
-                a = v - b
-                low = a if low is None else low + a
-                high = b if high is None else high + b
-            zsum[u, 0, y, at_rows, :] = low.astype(BF)
-            zsum[u, 1, y, at_rows, :] = high.astype(BF)
+            r = rows16(lax.rem(i, NZ))
+            low, high = binned([rbuf[k, y, r, :] for k in range(NX)], xmarks)
+            zsum[0, y, r, :] = low
+            zsum[1, y, r, :] = high
             return 0
 
         lax.fori_loop(0, 2 * NZ, body, 0)
 
-    def plus(a, b):
-        return (a.astype(F32) + b.astype(F32)).astype(BF)
-
-    def ring(u, s):
-        for way, (peer, sign) in enumerate(((zright, 1), (zleft, -1))):
-            part = rows16(around(z, sign * (4 - s), NZ))
-            if s == 0:
-                c = remote(
-                    zsum.at[u, :, way, part, :],
-                    zin.at[u, way, 0, :, way],
-                    zs.at[u, way, 0],
-                    zr.at[u, way, 0],
-                    peer,
-                )
-            else:
-                steps[u, way].wait_recv()
-                if s == 1:
-                    zin[u, way, 0, :, way] = plus(
-                        zin[u, way, 0, :, way], zsum[u, :, way, part, :]
-                    )
-                    zin[u, way, 0, :, 1 - way] = zsum[u, :, 1 - way, part, :]
-                else:
-                    zin[u, way, s - 1] = plus(zin[u, way, s - 1], zsum[u, :, :, part, :])
-                c = remote(
-                    zin.at[u, way, s - 1],
-                    zin.at[u, way, s],
-                    zs.at[u, way, s],
-                    zr.at[u, way, s],
-                    peer,
-                )
-            steps[u, way] = c
-            sends.append(c)
-
-    def total(u, y):
-        part = rows16(z)
-        v = zsum[u, :, y, part, :].astype(F32)
-        v = v + zin[u, 0, 3, :, y].astype(F32)
-        return v + zin[u, 1, 3, :, y].astype(F32)
+    def first(u):
+        zsum, dbuf, tbuf, hbuf = bufs[u][1:5]
+        stepping[u] = []
+        for i, by in enumerate((1, -1)):
+            a = remote(
+                zsum.at[:, :, rows16(around(z, 3 * by, NZ)), :],
+                tbuf.at[i],
+                zs.at[u, i],
+                zr.at[u, i],
+                zline[by % NZ - 1],
+            )
+            b = remote(
+                zsum.at[:, i, rows16(around(z, 4, NZ)), :],
+                hbuf.at[i],
+                zs.at[u, 2 + i],
+                zr.at[u, 2 + i],
+                zline[2 * by % NZ - 1],
+            )
+            stepping[u].append((a, b))
+            sends.extend([a, b])
+        for i, by in enumerate((1, -1)):
+            a = remote(
+                zsum.at[:, :, rows16(around(z, by, NZ)), :],
+                dbuf.at[i],
+                zs.at[u, 4 + i],
+                zr.at[u, 4 + i],
+                zline[by % NZ - 1],
+            )
+            stepping[u].append(a)
+            sends.append(a)
+
+    def second(u):
+        zsum, dbuf, tbuf, hbuf, obuf, ebuf = bufs[u][1:7]
+        waits = stepping[u][2:]
+        for i, by in enumerate((1, -1)):
+            for c in stepping[u][i]:
+                c.wait_recv()
+            part = rows16(around(z, 2 * by, NZ))
+            for y in range(2):
+                v = zsum[:, y, part, :].astype(F32) + tbuf[i, :, y].astype(F32)
+                if y == i:
+                    v = v + hbuf[i].astype(F32)
+                obuf[i, :, y] = v.astype(BF)
+            a = remote(
+                obuf.at[i], ebuf.at[i], zs.at[u, 6 + i], zr.at[u, 6 + i], zline[2 * by % NZ - 1]
+            )
+            waits.append(a)
+            sends.append(a)
+        stepping[u] = waits
 
     def swap(u):
-        steps[u, 0].wait_recv()
-        steps[u, 1].wait_recv()
-        ysend[u] = total(u, 1 - h).astype(BF)
-        cross[u] = remote(ysend.at[u], yin.at[u], ys.at[u], yr.at[u], over)
+        for c in stepping[u]:
+            c.wait_recv()
+        keep, ysend, yin = ends[u]
+
+        def total(y):
+            if u == n:
+                v = fsum[:, y, x].astype(F32)
+                for d in range(1, NX):
+                    v = v + fgot[d, :, y].astype(F32)
+                return v
+            zsum, dbuf, ebuf = bufs[u][1], bufs[u][2], bufs[u][6]
+            v = zsum[:, y, rows16(z), :].astype(F32)
+            for b in (dbuf, ebuf):
+                v = v + b[0, :, y].astype(F32) + b[1, :, y].astype(F32)
+            return v
+
+        ysend[...] = total(1 - h).astype(BF)
+        cross[u] = remote(ysend, yin, ys.at[u], yr.at[u], over)
         sends.append(cross[u])
-        keep[u] = total(u, h)
+        keep[...] = total(h)
 
     def finish(u):
-        w, c = todo[u]
+        w, c0, width = order[u] if u < n else FLIP
+        c = pl.ds(c0, width)
+        keep, ysend, yin = ends[u]
         cross[u].wait_recv()
         out = outs[w]
-        out[2 * h, :, c] = keep[u, h]
-        out[1, :, c] = keep[u, 1 - h] + yin[u, h].astype(F32)
-        out[2 - 2 * h, :, c] = yin[u, 1 - h].astype(F32)
+        out[2 * h, :, c] = keep[h]
+        out[1, :, c] = keep[1 - h] + yin[h].astype(F32)
+        out[2 - 2 * h, :, c] = yin[1 - h].astype(F32)
+
+    def flip_spread():
+        w, c0, width = FLIP
+        g, c = grads[w], pl.ds(c0, width)
+        arriving[n] = []
+        for d in (4, 3, 5, 2, 6, 1, 7):
+            a = remote(
+                g.at[:, :, rows16(around(z, d, NZ)), c],
+                fin.at[d],
+                gs.at[d],
+                gr.at[d],
+                zline[d - 1],
+            )
+            arriving[n].append(a)
+            sends.append(a)
+        a = pltpu.make_async_copy(g.at[:, :, rows16(z), c], fin.at[0], own.at[n])
+        a.start()
+        arriving[n].append(a)
+
+    def flip_second():
+        for c in arriving[n][:-1]:
+            c.wait_recv()
+        arriving[n][-1].wait()
+        marks = [flags[h * HALF + x * NZ + around(z, -d, NZ)].astype(F32) for d in range(NZ)]
+
+        def body(i, _):
+            y = lax.div(i, NX)
+            k = lax.rem(i, NX)
+            low, high = binned([fin[d, y, k] for d in range(NZ)], marks)
+            fsum[0, y, k] = low
+            fsum[1, y, k] = high
+            return 0
+
+        lax.fori_loop(0, 2 * NX, body, 0)
+        stepping[n] = []
+        for d in (2, 1, 3):
+            a = remote(
+                fsum.at[:, :, around(x, d, NX)], fgot.at[d], fs.at[d], fr.at[d], xline[d - 1]
+            )
+            stepping[n].append(a)
+            sends.append(a)
 
     yx = h * NX + x
     feats = res.shape[1] // 4
@@ -493,30 +588,27 @@
 
     spread(0)
     sums_out()
+    flip_spread()
     spread(1)
-    pass_on(0)
     for u in range(n):
+        arrive(u)
         if u + 2 < n:
             spread(u + 2)
-        if u + 1 < n:
-            pass_on(u + 1)
         bins(u)
-        ring(u, 0)
+        first(u)
         if u > 0:
-            ring(u - 1, 2)
-        ring(u, 1)
-        if u > 0:
-            ring(u - 1, 3)
             swap(u - 1)
-        if u == HOOKS[4]:
+        second(u)
+        if u == 0:
             widen()
-        if u == HOOKS[5]:
+        elif u == 2:
             homeward()
-    ring(n - 1, 2)
-    ring(n - 1, 3)
+            flip_second()
+        elif u == 4:
+            swap(n)
     swap(n - 1)
-    for u in range(n):
-        finish(u)
+    for u in range(n + 1):
+        finish((n + u) % (n + 1))
     stage["zl"].wait()
     for c in stage["z"]:
         c.wait_recv()
@@ -529,37 +621,57 @@
     cols = gg.shape[1]
     rows = res.shape[0]
     feats = res.shape[1] // 4
-    n = 3 * SPLIT
-    wide = cols // SPLIT
+    n = len(UNITS)
     shape = (2, NX, 16 * NZ, cols)
     vm = pl.BlockSpec(memory_space=pltpu.VMEM)
     hbm = pl.BlockSpec(memory_space=pl.ANY)
     dma = pltpu.SemaphoreType.DMA
     out = jax.ShapeDtypeStruct((3, 16, cols), F32)
     back = jax.ShapeDtypeStruct((2 * NX, NZ, SLOT, 2 * feats), BF)
+    bufs = []
+    for _, _, wide in UNITS[::-1]:
+        bufs += [
+            pltpu.VMEM((NX, 2, 16 * NZ, wide), BF),
+            pltpu.VMEM((2, 2, 16 * NZ, wide), BF),
+            pltpu.VMEM((2, 2, 2, 16, wide), BF),
+            pltpu.VMEM((2, 2, 2, 16, wide), BF),
+            pltpu.VMEM((2, 2, 16, wide), BF),
+            pltpu.VMEM((2, 2, 2, 16, wide), BF),
+            pltpu.VMEM((2, 2, 2, 16, wide), BF),
+            pltpu.VMEM((2, 16, wide), F32),
+            pltpu.VMEM((2, 16, wide), BF),
+            pltpu.VMEM((2, 16, wide), BF),
+        ]
+    wide = FLIP[2]
+    bufs += [
+        pltpu.VMEM((NZ, 2, NX, 16, wide), BF),
+        pltpu.VMEM((2, 2, NX, 16, wide), BF),
+        pltpu.VMEM((NX, 2, 2, 16, wide), BF),
+        pltpu.VMEM((2, 16, wide), F32),
+        pltpu.VMEM((2, 16, wide), BF),
+        pltpu.VMEM((2, 16, wide), BF),
+    ]
     return pl.pallas_call(
         reduce_kernel,
         out_shape=(out, out, out, back),
         in_specs=[pl.BlockSpec(memory_space=pltpu.SMEM)] + [hbm] * 5 + [vm],
         out_specs=[vm] * 3 + [hbm],
-        scratch_shapes=[
-            pltpu.VMEM((n, 4, 2, 16 * NZ, wide), BF),
-            pltpu.VMEM((n, 2, 16 * NZ, wide), BF),
-            pltpu.VMEM((n, 2, 2, 16 * NZ, wide), BF),
-            pltpu.VMEM((n, 2, 4, 2, 2, 16, wide), BF),
-            pltpu.VMEM((n, 2, 16, wide), F32),
-            pltpu.VMEM((n, 2, 16, wide), BF),
-            pltpu.VMEM((n, 2, 16, wide), BF),
+        scratch_shapes=bufs
+        + [
             pltpu.VMEM((4, 2, rows, feats), BF),
             pltpu.VMEM((2 * HALF, SLOT, 2 * feats), BF),
             pltpu.VMEM((NZ, 2 * NX, SLOT, 2 * feats), BF),
-            dma((n,)),
-            dma((n,)),
-            dma((n, 2, 4)),
-            dma((n, 2, 4)),
-            dma((n, 6)),
-            dma((n, 6)),
-            dma((n,)),
+            dma((n + 1,)),
+            dma((n + 1,)),
+            dma((n, 8)),
+            dma((n, 8)),
+            dma((n, 4)),
+            dma((n, 4)),
+            dma((n + 1,)),
+            dma((4,)),
+            dma((4,)),
+            dma((8,)),
+            dma((8,)),
             dma((16,)),
             dma((16,)),
             dma((2,)),

time: 287 us -> 248 us (0.86)
  Pallas kernels: 256 us -> 219 us
    pallas_call x1, Pallas kernels: 129 us -> 105 us  [reduce_all(): pl.pallas_call(reduce_kernel, out_shape=(out, out, out, back), in_specs=[...]
    pallas_call x1, Pallas kernels: 127 us -> 114 us  [gather_all(): pl.pallas_call(gather_kernel, out_shape=(out, out, out, full, full, close...]
where the time goes in v3:
time: 248 us; the launch traced here: 246 us
  Pallas kernels  219 us (88%)
  matrix products  17.3 us (7%)
  local copies, waits for them, and re-layouts  6.17 us (2%)
  between operations  2.78 us (1%)
    pallas_call x1, Pallas kernels, gather_all(): pl.pallas_call(gather_kernel, out_shape=(out, out, out, full, full, close...  114 us
    pallas_call x1, Pallas kernels, reduce_all(): pl.pallas_call(reduce_kernel, out_shape=(out, out, out, back), in_specs=[...  105 us

profile of v3, /device:TPU:16, one launch (start us, length us, event | category | flops | bytes accessed | tf_op | source)
XLA Modules:
  0.0 246.3 jit_solution(17487775927829233861)
XLA Ops:
  0.6 1.3 fusion.16
  4.0 0.7 select_add_fusion
  4.7 0.1 convert_reduce_fusion
  4.8 0.1 broadcast_in_dim.41
  4.9 0.2 fusion.4
  5.1 1.7 fusion.2
  6.9 0.0 copy-start
  6.9 0.0 copy-start.1
  6.9 0.0 copy-start.2
  6.9 0.1 select_convert_fusion.tok
  7.0 0.7 copy-done
  7.8 0.0 copy-done.1
  7.8 0.0 copy-done.2
  7.9 114.3 %gather_all.1 = (bf16[2,4,128,1024]{3,2,1,0:T(8,128)(2,1)S(1)}, bf16[2,4,128,1024]{3,2,1,0:T(8,128)(2,1)}, bf16[2,4,128,1024]{3,2,1,0:T(8,128)(2,1)}, bf16[384,1...) custom-call(s32[64]{0:T(128)S(1)} %fusion.12.flags, ...), custom_call_target="tpu_custom_call" | custom-call | bytes 200000000 | tf_op jit(solution)/shard_map/gather_all/pallas_call | solution.py:295
  122.2 2.6 %fusion.17 = f32[384,1024]{1,0:T(8,128)S(1)} fusion(bf16[384,1024]{1,0:T(8,128)(2,1)S(1)} %get-tuple-element.16, bf16[1024,1024]{1,0:T(8,128)(2,1)} %bitcast.38), kind=kOutput, calls=%fused_computation.42 | convolution fusion | flops 805306368 | bytes 4456448 | tf_op jit(solution)/shard_map/dot_general | solution.py:697
  124.8 0.0 copy-start.4
  124.8 1.0 fusion.18
  125.8 0.6 copy-done.4
  126.3 1.5 multiply_convert_fusion
  127.9 1.0 fusion.19
  128.9 0.0 copy-start.3
  129.0 1.0 add_convert_fusion.dx
  130.0 0.6 copy-done.3
  130.5 1.0 convolution_convert_fusion.3.res
  131.6 2.6 %convolution_convert_fusion = bf16[1024,1024]{1,0:T(8,128)(2,1)} fusion(bf16[384,1024]{1,0:T(8,128)(2,1)S(1)} %get-tuple-element.16, bf16[384,1024]{1,0:T(8,128)(2,1)S(1)} %get-tuple-element.25), kind=kOutput, calls=%fused_computation.1 | convolution fusion | flops 806354944 | bytes 3670016 | tf_op jit(solution)/shard_map/dot_general | solution.py:705
  134.2 1.3 convolution_convert_fusion.2
  135.5 2.6 %convolution_convert_fusion.1 = bf16[1024,1024]{1,0:T(8,128)(2,1)} fusion(bf16[384,1024]{1,0:T(8,128)(2,1)S(1)} %get-tuple-element.15, bf16[384,1024]{1,0:T(8,128)(2,1)S(1)} %get-tuple-element.27), kind=kOutput, calls=%fused_computation.2 | convolution fusion | flops 806354944 | bytes 3670016 | tf_op jit(solution)/shard_map/dot_general | solution.py:704
  138.1 104.8 %reduce_all.1 = (f32[3,16,1024]{2,1,0:T(8,128)S(1)}, f32[3,16,1024]{2,1,0:T(8,128)S(1)}, f32[3,16,1024]{2,1,0:T(8,128)S(1)}, bf16[8,8,16,512]{3,2,1,0:T(8,128)(2,1)S(1)}) custom-call(s32[64]{0:T(128)S(1)} %fusion.12.flags, bf16[2,4,128,1024]{3,2,1,0:T(8,128)(2,1)S(1)} %bitcast.31, bf16[2,4,128,1024]{3,2,1,0:T(8,128)(2,1)} %bitcast.36, ...), custom_call_target="tpu_custom_call" | custom-call | bytes 200000000 | tf_op jit(solution)/shard_map/reduce_all/pallas_call | solution.py:654
  242.9 0.6 fusion.3
  243.5 0.8 fusion.15
  244.3 0.7 copy.16
  244.9 0.7 copy.17
  245.6 0.7 copy.18
  (3 shorter events, 0.0 us)
Async XLA Ops:
  6.9 0.9 copy-start
  6.9 0.9 copy-start.1
  6.9 1.0 copy-start.2
  124.8 1.6 copy-start.4
  128.9 1.6 copy-start.3

commit v4 on v3

--- a/solution.py
+++ b/solution.py
@@ -112,17 +112,16 @@
     def first(u):
         cross[u].wait_recv()
         v = zbuf[u].at[:, :, rows16(z), :]
-        near[u] = [
-            remote(v, v, zs.at[u, i], zr.at[u, i], zline[d % NZ - 1])
-            for i, d in ((2, 2), (3, -2), (0, 1), (1, -1))
-        ]
-        sends.extend(near[u])
+        hops = ((2, 2), (3, -2), (0, 1), (1, -1))
+        near[u] = {
+            i: remote(v, v, zs.at[u, i], zr.at[u, i], zline[d % NZ - 1]) for i, d in hops
+        }
+        sends.extend(near[u].values())
 
     def second(u):
-        ahead, behind = near[u][:2]
-        later[u] = near[u][2:]
-        for i, (got, by) in enumerate(((ahead, 1), (behind, -1))):
-            got.wait_recv()
+        later[u] = [near[u][0], near[u][1]]
+        for i, by in enumerate((1, -1)):
+            near[u][2 + i].wait_recv()
             chunk = rows16(around(z, -2 * by, NZ))
             v = zbuf[u].at[:, :, chunk, :]
             a = remote(v, v, zs.at[u, 4 + i], zr.at[u, 4 + i], zline[by % NZ - 1])
@@ -174,41 +173,40 @@
     yx = h * NX + x
     stage = {}
 
-    def tokens_z():
-        stage["z"] = []
-        for d in range(1, NZ):
-            to = around(z, d, NZ)
-            stage["z"].append(
-                remote(tok.at[:, to], tmid.at[z], ts.at[d], tr.at[d], zline[d - 1])
-            )
-        a = pltpu.make_async_copy(tok.at[:, z], tmid.at[z], tl.at[0])
-        a.start()
-        stage["zl"] = a
-
     def tokens_plane():
-        stage["zl"].wait()
-        for c in stage["z"]:
-            c.wait_recv()
-        sends.extend(stage["z"])
         stage["p"] = []
-        to = rows.at[pl.ds(yx * NZ, NZ)]
         for d in range(1, 2 * NX):
             k, peer = plane[d - 1]
             stage["p"].append(
-                remote(tmid.at[:, k], to, ts.at[NZ + d], tr.at[NZ + d], peer)
-            )
-        a = pltpu.make_async_copy(tmid.at[:, yx], to, tl.at[1])
+                remote(tok.at[k], tmid.at[yx], ts.at[NZ + d], tr.at[NZ + d], peer)
+            )
+        sends.extend(stage["p"])
+        a = pltpu.make_async_copy(tok.at[yx], tmid.at[yx], tl.at[1])
         a.start()
         stage["pl"] = a
 
-    def compact():
+    def tokens_z():
         stage["pl"].wait()
         for c in stage["p"]:
             c.wait_recv()
-        sends.extend(stage["p"])
-        groups = rows.shape[0]
+        stage["z"] = []
+        for d in (4, 3, 5, 2, 6, 1, 7):
+            to = around(z, d, NZ)
+            stage["z"].append(
+                remote(tmid.at[:, to], rows.at[:, z], ts.at[d], tr.at[d], zline[d - 1])
+            )
+        sends.extend(stage["z"])
+        a = pltpu.make_async_copy(tmid.at[:, z], rows.at[:, z], tl.at[0])
+        a.start()
+        stage["zl"] = a
+
+    def compact():
+        stage["zl"].wait()
+        for c in stage["z"]:
+            c.wait_recv()
+        groups = 2 * HALF
         spot = lax.broadcasted_iota(jnp.int32, (groups, SLOT, 128), 1)
-        head = rows[:, :, 0:128].astype(F32)
+        head = rows[:, :, :, 0:128].reshape(groups, SLOT, 128).astype(F32)
         count = jnp.sum(jnp.where(spot == CAP, head, 0.0), axis=1)
         i = lax.broadcasted_iota(jnp.int32, (groups, groups), 0)
         j = lax.broadcasted_iota(jnp.int32, (groups, groups), 1)
@@ -221,9 +219,9 @@
         for b in range(close.shape[1] // 128):
             hit = rank == (lane + b * 128).astype(F32)
             close[:, b * 128 : (b + 1) * 128] = jnp.where(hit, 1.0, 0.0).astype(BF)
-        feats = rows.shape[2] // 2
+        feats = rows.shape[3] // 2
         for b in range(2):
-            part = rows[:, :, b * feats : (b + 1) * feats].reshape(groups * SLOT, feats)
+            part = rows[:, :, :, b * feats : (b + 1) * feats].reshape(groups * SLOT, feats)
             picked = lax.dot_general(
                 close[...], part, (((0,), (0,)), ((), ())), preferred_element_type=F32
             )
@@ -251,20 +249,19 @@
 
     for u in range(n + 1):
         begin(u)
+    tokens_plane()
     first(0)
     flip_first()
     second(0)
     first(1)
-    tokens_z()
     spread(0)
     second(1)
     first(2)
+    tokens_z()
     spread(1)
     second(2)
-    flip_second()
     first(3)
     spread(2)
-    tokens_plane()
     second(3)
     first(4)
     spread(3)
@@ -273,8 +270,9 @@
     compact()
     spread(4)
     second(5)
+    flip_second()
+    spread(5)
     share()
-    spread(5)
     for c in waits:
         c.wait_recv()
     for c in sends:
@@ -302,8 +300,8 @@
         + [
             pltpu.VMEM((2, 2, NX, 16, FLIP[2]), BF),
             pltpu.VMEM((NZ, 2, NX, 16, FLIP[2]), BF),
-            pltpu.VMEM((NZ, 2 * NX, SLOT, 2 * feats), BF),
-            pltpu.VMEM((2 * HALF, SLOT, 2 * feats), BF),
+            pltpu.VMEM((2 * NX, NZ, SLOT, 2 * feats), BF),
+            pltpu.VMEM((2 * NX, NZ, SLOT, 2 * feats), BF),
             pltpu.VMEM((2, rows, feats), BF),
             dma((n + 1,)),
             dma((n + 1,)),
@@ -548,71 +546,92 @@
         for c in stage["m"]:
             c.wait_recv()
         sends.extend(stage["m"])
-        groups = spread_rows.shape[0]
         for b in range(2):
             v = pin[3, b].astype(F32)
             for i in range(3):
                 v = v + pin[i, b].astype(F32)
             v = jnp.dot(close[...], v.astype(BF), preferred_element_type=F32).astype(BF)
-            spread_rows[:, :, b * feats : (b + 1) * feats] = v.reshape(groups, SLOT, feats)
+            spread_rows[:, :, :, b * feats : (b + 1) * feats] = v.reshape(
+                2 * NX, NZ, SLOT, feats
+            )
+        stage["z"] = []
+        for d in (4, 3, 5, 2, 6, 1, 7):
+            stage["z"].append(
+                remote(
+                    spread_rows.at[:, around(z, d, NZ)],
+                    tmid.at[z],
+                    ts.at[d],
+                    tr.at[d],
+                    zline[d - 1],
+                )
+            )
+        sends.extend(stage["z"])
+        a = pltpu.make_async_copy(spread_rows.at[:, z], tmid.at[z], tl.at[0])
+        a.start()
+        stage["zl"] = a
+
+    def homeward():
+        stage["zl"].wait()
+        for c in stage["z"]:
+            c.wait_recv()
         stage["p"] = []
         for d in range(1, 2 * NX):
             k, peer = plane[d - 1]
             stage["p"].append(
-                remote(
-                    spread_rows.at[pl.ds(k * NZ, NZ)],
-                    tmid.at[:, yx],
-                    ts.at[NZ + d],
-                    tr.at[NZ + d],
-                    peer,
-                )
-            )
-        a = pltpu.make_async_copy(spread_rows.at[pl.ds(yx * NZ, NZ)], tmid.at[:, yx], tl.at[0])
+                remote(tmid.at[:, k], back.at[yx], ts.at[NZ + d], tr.at[NZ + d], peer)
+            )
+        sends.extend(stage["p"])
+        a = pltpu.make_async_copy(tmid.at[:, yx], back.at[yx], tl.at[1])
         a.start()
         stage["pl"] = a
 
-    def homeward():
-        stage["pl"].wait()
-        for c in stage["p"]:
-            c.wait_recv()
-        sends.extend(stage["p"])
-        stage["z"] = []
-        for d in range(1, NZ):
-            to = around(z, d, NZ)
-            stage["z"].append(
-                remote(tmid.at[to], back.at[:, z], ts.at[d], tr.at[d], zline[d - 1])
-            )
-        a = pltpu.make_async_copy(tmid.at[z], back.at[:, z], tl.at[1])
-        a.start()
-        stage["zl"] = a
-
+    sums_out()
     spread(0)
-    sums_out()
     flip_spread()
     spread(1)
-    for u in range(n):
-        arrive(u)
-        if u + 2 < n:
-            spread(u + 2)
-        bins(u)
-        first(u)
-        if u > 0:
-            swap(u - 1)
-        second(u)
-        if u == 0:
-            widen()
-        elif u == 2:
-            homeward()
-            flip_second()
-        elif u == 4:
-            swap(n)
+    spread(2)
+    spread(3)
+    spread(4)
+    spread(5)
+    arrive(0)
+    bins(0)
+    first(0)
+    widen()
+    second(0)
+    arrive(1)
+    bins(1)
+    first(1)
+    swap(0)
+    second(1)
+    arrive(2)
+    bins(2)
+    first(2)
+    swap(1)
+    second(2)
+    homeward()
+    flip_second()
+    arrive(3)
+    bins(3)
+    first(3)
+    swap(2)
+    second(3)
+    arrive(4)
+    bins(4)
+    first(4)
+    swap(3)
+    second(4)
+    swap(n)
+    arrive(5)
+    bins(5)
+    first(5)
+    swap(4)
+    second(5)
     swap(n - 1)
     for u in range(n + 1):
         finish((n + u) % (n + 1))
-    stage["zl"].wait()
-    for c in stage["z"]:
+    stage["pl"].wait()
+    for c in stage["p"]:
         c.wait_recv()
-        c.wait_send()
     for c in sends:
         c.wait_send()
 
@@ -659,7 +678,7 @@
         scratch_shapes=bufs
         + [
             pltpu.VMEM((4, 2, rows, feats), BF),
-            pltpu.VMEM((2 * HALF, SLOT, 2 * feats), BF),
+            pltpu.VMEM((2 * NX, NZ, SLOT, 2 * feats), BF),
             pltpu.VMEM((NZ, 2 * NX, SLOT, 2 * feats), BF),
             dma((n + 1,)),
             dma((n + 1,)),

time: 248 us -> 230 us (0.927)
  Pallas kernels: 219 us -> 203 us
    pallas_call x1, Pallas kernels: 105 us -> 95.8 us  [reduce_all(): pl.pallas_call(reduce_kernel, out_shape=(out, out, out, back), in_specs=[...]
    pallas_call x1, Pallas kernels: 114 us -> 107 us  [gather_all(): pl.pallas_call(gather_kernel, out_shape=(out, out, out, full, full, close...]
where the time goes in v4:
time: 230 us
  Pallas kernels  203 us (88%)
  matrix products  17.3 us (8%)
  local copies, waits for them, and re-layouts  6.17 us (3%)
  between operations  2.78 us (1%)
    pallas_call x1, Pallas kernels, gather_all(): pl.pallas_call(gather_kernel, out_shape=(out, out, out, full, full, close...  107 us
    pallas_call x1, Pallas kernels, reduce_all(): pl.pallas_call(reduce_kernel, out_shape=(out, out, out, back), in_specs=[...  95.8 us

profile of v4, /device:TPU:16, one launch (start us, length us, event | category | flops | bytes accessed | tf_op | source)
XLA Modules:
  0.0 230.2 jit_solution(17340400969230763243)
XLA Ops:
  0.6 1.3 fusion.16
  4.0 0.7 select_add_fusion
  4.7 0.1 convert_reduce_fusion
  4.8 0.1 broadcast_in_dim.41
  4.9 0.2 fusion.4
  5.1 1.7 fusion.2
  6.9 0.0 copy-start
  6.9 0.0 copy-start.1
  6.9 0.0 copy-start.2
  6.9 0.1 select_convert_fusion.tok
  7.0 0.7 copy-done
  7.8 0.0 copy-done.1
  7.8 0.0 copy-done.2
  7.9 107.1 %gather_all.1 = (bf16[2,4,128,1024]{3,2,1,0:T(8,128)(2,1)S(1)}, bf16[2,4,128,1024]{3,2,1,0:T(8,128)(2,1)}, bf16[2,4,128,1024]{3,2,1,0:T(8,128)(2,1)}, bf16[384,1...) custom-call(s32[64]{0:T(128)S(1)} %fusion.12.flags, ...), custom_call_target="tpu_custom_call" | custom-call | bytes 200000000 | tf_op jit(solution)/shard_map/gather_all/pallas_call | solution.py:293
  115.0 2.6 %fusion.17 = f32[384,1024]{1,0:T(8,128)S(1)} fusion(bf16[384,1024]{1,0:T(8,128)(2,1)S(1)} %get-tuple-element.16, bf16[1024,1024]{1,0:T(8,128)(2,1)} %bitcast.38), kind=kOutput, calls=%fused_computation.42 | convolution fusion | flops 805306368 | bytes 4456448 | tf_op jit(solution)/shard_map/dot_general | solution.py:716
  117.5 0.0 copy-start.4
  117.6 1.0 fusion.18
  118.5 0.6 copy-done.4
  119.1 1.5 multiply_convert_fusion
  120.7 1.0 fusion.19
  121.7 0.0 copy-start.3
  121.7 1.0 add_convert_fusion.dx
  122.8 0.6 copy-done.3
  123.3 1.0 convolution_convert_fusion.3.res
  124.4 2.6 %convolution_convert_fusion = bf16[1024,1024]{1,0:T(8,128)(2,1)} fusion(bf16[384,1024]{1,0:T(8,128)(2,1)S(1)} %get-tuple-element.16, bf16[384,1024]{1,0:T(8,128)(2,1)S(1)} %get-tuple-element.25), kind=kOutput, calls=%fused_computation.1 | convolution fusion | flops 806354944 | bytes 3670016 | tf_op jit(solution)/shard_map/dot_general | solution.py:724
  127.0 1.3 convolution_convert_fusion.2
  128.3 2.6 %convolution_convert_fusion.1 = bf16[1024,1024]{1,0:T(8,128)(2,1)} fusion(bf16[384,1024]{1,0:T(8,128)(2,1)S(1)} %get-tuple-element.15, bf16[384,1024]{1,0:T(8,128)(2,1)S(1)} %get-tuple-element.27), kind=kOutput, calls=%fused_computation.2 | convolution fusion | flops 806354944 | bytes 3670016 | tf_op jit(solution)/shard_map/dot_general | solution.py:723
  130.9 95.8 %reduce_all.1 = (f32[3,16,1024]{2,1,0:T(8,128)S(1)}, f32[3,16,1024]{2,1,0:T(8,128)S(1)}, f32[3,16,1024]{2,1,0:T(8,128)S(1)}, bf16[8,8,16,512]{3,2,1,0:T(8,128)(2,1)S(1)}) custom-call(s32[64]{0:T(128)S(1)} %fusion.12.flags, bf16[2,4,128,1024]{3,2,1,0:T(8,128)(2,1)S(1)} %bitcast.31, bf16[2,4,128,1024]{3,2,1,0:T(8,128)(2,1)} %bitcast.36, ...), custom_call_target="tpu_custom_call" | custom-call | bytes 200000000 | tf_op jit(solution)/shard_map/reduce_all/pallas_call | solution.py:673
  226.7 0.6 fusion.3
  227.4 0.8 fusion.15
  228.1 0.7 copy.16
  228.8 0.7 copy.17
  229.5 0.7 copy.18
  (3 shorter events, 0.0 us)
Async XLA Ops:
  6.9 0.9 copy-start
  6.9 0.9 copy-start.1
  6.9 1.0 copy-start.2
  117.5 1.6 copy-start.4
  121.7 1.6 copy-start.3

commit v5 on v4

--- a/solution.py
+++ b/solution.py
@@ -77,15 +77,29 @@
     return at, zline, plane, parts
 
 
+def starts(counts, rows):
+    b = lax.div(counts[0], rows)
+    return b, lax.div(counts[0] + counts[1], rows)
+
+
+def flag_of(begin, g):
+    b, c = begin
+    mod = (g >= b).astype(jnp.int32) + (g >= c).astype(jnp.int32)
+    return jnp.clip(mod - lax.div(g, HALF), 0, 1)
+
+
 def lanes_of(p, feats):
     return pl.ds(pl.multiple_of(p * feats, 128), feats)
 
 
-def gather_kernel(flags, wg, wu, wd, tok, og, ou, od, fx, fdy, close, *scratch):
+def gather_kernel(
+    counts, wg, wu, wd, xin, dyin, tags, target, og, ou, od, fx, fdy, close, position, *scratch
+):
     n = len(UNITS)
     zbuf, sbuf = scratch[:n], scratch[n : 2 * n]
-    fbuf, fsend, tmid, rows, mine = scratch[2 * n : 2 * n + 5]
-    ys, yr, zs, zr, xs, xr, own, fs, fr, gs, gr, ts, tr, tl, ms, mr, ml = scratch[2 * n + 5 :]
+    begins = starts(counts, xin.shape[0])
+    fbuf, fsend, tmid, rows, mine, tok = scratch[2 * n : 2 * n + 6]
+    ys, yr, zs, zr, xs, xr, own, fs, fr, gs, gr, ts, tr, tl, ms, mr, ml = scratch[2 * n + 6 :]
     p, h, x, z = place()
     at, zline, plane, parts = peers_of(p, h, x, z)
     over = at(1 - h, x, z)
@@ -136,7 +150,7 @@
         w, c0, width = UNITS[u]
         out = outs[w].at[:, x, :, pl.ds(c0, width)]
         for d in (2, 1, 3, 0):
-            f = flags[h * HALF + around(x, d, NX) * NZ + z]
+            f = flag_of(begins, h * HALF + around(x, d, NX) * NZ + z)
             sbuf[u][d] = zbuf[u][f]
             if d == 0:
                 a = pltpu.make_async_copy(sbuf[u].at[0], out, own.at[u])
@@ -159,7 +173,7 @@
         w, c0, width = FLIP
         out = outs[w].at[:, :, rows16(z), pl.ds(c0, width)]
         for d in (4, 3, 5, 2, 6, 1, 7, 0):
-            f = flags[h * HALF + x * NZ + around(z, d, NZ)]
+            f = flag_of(begins, h * HALF + x * NZ + around(z, d, NZ))
             fsend[d] = fbuf[f]
             if d == 0:
                 a = pltpu.make_async_copy(fsend.at[0], out, own.at[n])
@@ -172,6 +186,36 @@
 
     yx = h * NX + x
     stage = {}
+
+    def address():
+        count = xin.shape[0]
+        groups = 2 * HALF
+        wide = groups * SLOT
+        kind = tags[...]
+        base = jnp.where(kind == 0, 0, jnp.where(kind == 1, begins[0], begins[1]))
+        dest = base + target[...]
+        spread_dest = jnp.broadcast_to(dest.astype(F32), (count, count))
+        i = lax.broadcasted_iota(jnp.int32, (count, count), 0)
+        j = lax.broadcasted_iota(jnp.int32, (count, count), 1)
+        same = (spread_dest == spread_dest.T) & (i < j)
+        slot = jnp.sum(jnp.where(same, 1.0, 0.0), axis=0, keepdims=True)
+        place_row = dest * SLOT + slot.astype(jnp.int32)
+        position[...] = place_row
+        i = lax.broadcasted_iota(jnp.int32, (wide, count), 0)
+        into = jnp.where(i == place_row, 1.0, 0.0).astype(BF)
+        feats = xin.shape[1]
+        i = lax.broadcasted_iota(jnp.int32, (groups, count), 0)
+        goes = jnp.where(i == dest, 1.0, 0.0).astype(BF)
+        sent = jnp.dot(goes, jnp.ones((count, feats), BF), preferred_element_type=F32)
+        spot = lax.broadcasted_iota(jnp.int32, (groups, SLOT, feats), 1)
+        for b, v in enumerate((xin, dyin)):
+            part = jnp.dot(into, v[...], preferred_element_type=F32)
+            part = part.reshape(groups, SLOT, feats)
+            if b == 0:
+                part = jnp.where(spot >= CAP, sent[:, None, :], part)
+            tok[:, :, :, b * feats : (b + 1) * feats] = part.astype(BF).reshape(
+                2 * NX, NZ, SLOT, feats
+            )
 
     def tokens_plane():
         stage["p"] = []
@@ -249,9 +293,10 @@
 
     for u in range(n + 1):
         begin(u)
-    tokens_plane()
     first(0)
     flip_first()
+    address()
+    tokens_plane()
     second(0)
     first(1)
     spread(0)
@@ -281,8 +326,9 @@
         c.wait()
 
 
-def gather_all(flags, wg, wu, wd, tok, rows, feats):
+def gather_all(counts, wg, wu, wd, tokens, cotangent, tags, target):
     cols = wg.shape[2]
+    rows, feats = tokens.shape
     n = len(UNITS)
     vm = pl.BlockSpec(memory_space=pltpu.VMEM)
     hbm = pl.BlockSpec(memory_space=pl.ANY)
@@ -292,9 +338,9 @@
     close = jax.ShapeDtypeStruct((2 * HALF * SLOT, rows), BF)
     return pl.pallas_call(
         gather_kernel,
-        out_shape=(out, out, out, full, full, close),
-        in_specs=[pl.BlockSpec(memory_space=pltpu.SMEM), vm, vm, vm, vm],
-        out_specs=[hbm] * 5 + [vm],
+        out_shape=(out, out, out, full, full, close, jax.ShapeDtypeStruct((1, rows), jnp.int32)),
+        in_specs=[pl.BlockSpec(memory_space=pltpu.SMEM)] + [vm] * 7,
+        out_specs=[hbm] * 5 + [vm] * 2,
         scratch_shapes=[pltpu.VMEM((2, 2, 16 * NZ, u[2]), BF) for u in UNITS]
         + [pltpu.VMEM((4, 2, 16 * NZ, u[2]), BF) for u in UNITS]
         + [
@@ -303,6 +349,7 @@
             pltpu.VMEM((2 * NX, NZ, SLOT, 2 * feats), BF),
             pltpu.VMEM((2 * NX, NZ, SLOT, 2 * feats), BF),
             pltpu.VMEM((2, rows, feats), BF),
+            pltpu.VMEM((2 * NX, NZ, SLOT, 2 * feats), BF),
             dma((n + 1,)),
             dma((n + 1,)),
             dma((n, 8)),
@@ -326,36 +373,63 @@
         ),
         cost_estimate=pl.CostEstimate(flops=0, bytes_accessed=200_000_000, transcendentals=0),
         name="gather_all",
-    )(flags, wg, wu, wd, tok.reshape(2 * NX, NZ, SLOT, 2 * feats))
-
-
-def reduce_kernel(flags, gg, gu, gd, res, dx, close, og, ou, od, back, *scratch):
+    )(counts, wg, wu, wd, tokens, cotangent, tags.reshape(1, rows), target.reshape(1, rows))
+
+
+def reduce_kernel(
+    counts, xf, dyf, dgate, dup, hidden, res, dx, close, og, ou, od, back, *scratch
+):
     n = len(UNITS)
     per = 10
     bufs = [scratch[per * u : per * u + per] for u in range(n)]
     ends = [b[7:] for b in bufs] + [scratch[per * n + 3 : per * n + 6]]
     fin, fsum, fgot = scratch[per * n : per * n + 3]
     pin, spread_rows, tmid = scratch[per * n + 6 : per * n + 9]
-    ys, yr, zs, zr, xs, xr, own, fs, fr, gs, gr, ts, tr, tl, ms, mr, ml = scratch[per * n + 9 :]
+    made = scratch[per * n + 9 : per * n + 10 + n]
+    ys, yr, zs, zr, xs, xr, own, fs, fr, gs, gr, ts, tr, tl, ms, mr, ml = scratch[
+        per * n + 10 + n :
+    ]
+    begins = starts(counts, xf.shape[0])
     p, h, x, z = place()
     at, zline, plane, parts = peers_of(p, h, x, z)
     over = at(1 - h, x, z)
     xline = [at(h, around(x, d, NX), z) for d in range(1, NX)]
     greet(zline + [q for _, q in plane] + [q for _, q in parts])
-    grads = (gg, gu, gd)
+    pairs = ((xf, dgate), (xf, dup), (dyf, hidden))
     outs = (og, ou, od)
     order = UNITS[::-1]
     sends = []
     arriving, stepping, cross, stage = {}, {}, {}, {}
 
+    def make(u):
+        w, c0, width = order[u] if u < n else FLIP
+        left, right = pairs[w]
+        deep = 32 * NZ
+
+        def body(i, _):
+            cut = pl.ds(pl.multiple_of(i * deep, deep), deep)
+            v = lax.dot_general(
+                left[:, cut],
+                right[:, c0 : c0 + width],
+                (((0,), (0,)), ((), ())),
+                preferred_element_type=F32,
+            ).astype(BF)
+            y = lax.div(i, 2)
+            k = lax.rem(i, 2) * 2
+            made[u][y, k] = v[: deep // 2]
+            made[u][y, k + 1] = v[deep // 2 :]
+            return 0
+
+        lax.fori_loop(0, 4, body, 0)
+
     def spread(u):
-        w, c0, width = order[u]
-        g, c = grads[w], pl.ds(c0, width)
+        make(u)
+        g = made[u]
         rbuf = bufs[u][0]
         arriving[u] = []
         for d in (2, 1, 3):
             a = remote(
-                g.at[:, around(x, d, NX), :, c],
+                g.at[:, around(x, d, NX)],
                 rbuf.at[d],
                 xs.at[u, d],
                 xr.at[u, d],
@@ -363,7 +437,7 @@
             )
             arriving[u].append(a)
             sends.append(a)
-        a = pltpu.make_async_copy(g.at[:, x, :, c], rbuf.at[0], own.at[u])
+        a = pltpu.make_async_copy(g.at[:, x], rbuf.at[0], own.at[u])
         a.start()
         arriving[u].append(a)
 
@@ -383,7 +457,7 @@
         return low.astype(BF), high.astype(BF)
 
     xmarks = [
-        flags[h * HALF + around(x, -d, NX) * NZ + z].astype(F32) for d in range(NX)
+        flag_of(begins, h * HALF + around(x, -d, NX) * NZ + z).astype(F32) for d in range(NX)
     ]
 
     def bins(u):
@@ -482,12 +556,12 @@
         out[2 - 2 * h, :, c] = yin[1 - h].astype(F32)
 
     def flip_spread():
-        w, c0, width = FLIP
-        g, c = grads[w], pl.ds(c0, width)
+        make(n)
+        g = made[n]
         arriving[n] = []
         for d in (4, 3, 5, 2, 6, 1, 7):
             a = remote(
-                g.at[:, :, rows16(around(z, d, NZ)), c],
+                g.at[:, :, rows16(around(z, d, NZ)), :],
                 fin.at[d],
                 gs.at[d],
                 gr.at[d],
@@ -495,7 +569,7 @@
             )
             arriving[n].append(a)
             sends.append(a)
-        a = pltpu.make_async_copy(g.at[:, :, rows16(z), c], fin.at[0], own.at[n])
+        a = pltpu.make_async_copy(g.at[:, :, rows16(z), :], fin.at[0], own.at[n])
         a.start()
         arriving[n].append(a)
 
@@ -503,7 +577,10 @@
         for c in arriving[n][:-1]:
             c.wait_recv()
         arriving[n][-1].wait()
-        marks = [flags[h * HALF + x * NZ + around(z, -d, NZ)].astype(F32) for d in range(NZ)]
+        marks = [
+            flag_of(begins, h * HALF + x * NZ + around(z, -d, NZ)).astype(F32)
+            for d in range(NZ)
+        ]
 
         def body(i, _):
             y = lax.div(i, NX)
@@ -636,12 +713,11 @@
         c.wait_send()
 
 
-def reduce_all(flags, gg, gu, gd, res, dx, close):
-    cols = gg.shape[1]
+def reduce_all(counts, xf, dyf, dgate, dup, hidden, res, dx, close):
+    cols = dgate.shape[1]
     rows = res.shape[0]
     feats = res.shape[1] // 4
     n = len(UNITS)
-    shape = (2, NX, 16 * NZ, cols)
     vm = pl.BlockSpec(memory_space=pltpu.VMEM)
     hbm = pl.BlockSpec(memory_space=pl.ANY)
     dma = pltpu.SemaphoreType.DMA
@@ -673,13 +749,16 @@
     return pl.pallas_call(
         reduce_kernel,
         out_shape=(out, out, out, back),
-        in_specs=[pl.BlockSpec(memory_space=pltpu.SMEM)] + [hbm] * 5 + [vm],
+        in_specs=[pl.BlockSpec(memory_space=pltpu.SMEM)] + [vm] * 5 + [hbm] * 2 + [vm],
         out_specs=[vm] * 3 + [hbm],
         scratch_shapes=bufs
         + [
             pltpu.VMEM((4, 2, rows, feats), BF),
             pltpu.VMEM((2 * NX, NZ, SLOT, 2 * feats), BF),
             pltpu.VMEM((NZ, 2 * NX, SLOT, 2 * feats), BF),
+        ]
+        + [pltpu.VMEM((2, NX, 16 * NZ, u[2]), BF) for u in UNITS[::-1] + (FLIP,)]
+        + [
             dma((n + 1,)),
             dma((n + 1,)),
             dma((n, 8)),
@@ -703,7 +782,7 @@
         ),
         cost_estimate=pl.CostEstimate(flops=0, bytes_accessed=200_000_000, transcendentals=0),
         name="reduce_all",
-    )(flags, gg.reshape(shape), gu.reshape(shape), gd.reshape(shape), res, dx, close)
+    )(counts, xf, dyf, dgate, dup, hidden, res, dx, close)
 
 
 def project_rows(x, dy, wg, wu, wd):
@@ -718,48 +797,23 @@
     dup = (dhidden * silu).astype(BF)
     dx = lax.dot_general(dgate, wg, (((1,), (1,)), ((), ())), preferred_element_type=F32)
     dx = dx + lax.dot_general(dup, wu, (((1,), (1,)), ((), ())), preferred_element_type=F32)
-    over_rows = (((0,), (0,)), ((), ()))
-    grad_g = lax.dot_general(x, dgate, over_rows, preferred_element_type=F32).astype(BF)
-    grad_u = lax.dot_general(x, dup, over_rows, preferred_element_type=F32).astype(BF)
-    grad_d = lax.dot_general(dy, hidden, over_rows, preferred_element_type=F32).astype(BF)
-    return out, dx, grad_g, grad_u, grad_d
+    return out.astype(BF), dx.astype(BF), hidden, dgate, dup
 
 
 def shards(tokens, cotangent, tags, counts, target, gate_weight, up_weight, down_weight):
-    groups = lax.axis_size("group")
-    rows, feats = tokens.shape
-    total = rows * groups
-    start_b = groups * counts[0] // total
-    start_c = groups * (counts[0] + counts[1]) // total
-    devices = jnp.arange(groups, dtype=jnp.int32)
-    device_mod = (devices >= start_b).astype(jnp.int32) + (devices >= start_c).astype(jnp.int32)
-    flags = device_mod - devices // HALF
-    base = jnp.where(tags == 0, 0, jnp.where(tags == 1, start_b, start_c))
-    dest = base + target
-    onehot = (dest[:, None] == devices[None, :]).astype(BF)
-    places = jnp.arange(rows, dtype=jnp.int32)
-    lower = (places[:, None] > places[None, :]).astype(BF)
-    earlier = jnp.dot(lower, onehot, preferred_element_type=F32)
-    slot = jnp.sum(earlier * onehot.astype(F32), axis=1).astype(jnp.int32)
-    sent = jnp.sum(onehot.astype(F32), axis=0)
-    position = dest * SLOT + slot
-    wide = groups * SLOT
-    lanes = jnp.arange(wide, dtype=jnp.int32)
-    both = jnp.concatenate([tokens, cotangent], axis=1)
-    into = (lanes[:, None] == position[None, :]).astype(BF)
-    send = jnp.dot(into, both, preferred_element_type=F32).reshape(groups, SLOT, 2 * feats)
-    tail = (jnp.arange(SLOT, dtype=jnp.int32) >= CAP)[None, :, None]
-    send = jnp.where(tail, sent[:, None, None], send).astype(BF).reshape(wide, 2 * feats)
-    w_gate, w_up, w_down, full_x, full_dy, close = gather_all(
-        flags, gate_weight, up_weight, down_weight, send, rows, feats
+    feats = tokens.shape[1]
+    w_gate, w_up, w_down, full_x, full_dy, close, position = gather_all(
+        counts, gate_weight, up_weight, down_weight, tokens, cotangent, tags, target
     )
     depth = full_x.shape[1]
     w_gate, w_up, w_down = (w.reshape(depth, -1) for w in (w_gate, w_up, w_down))
-    out, dx, grad_g, grad_u, grad_d = project_rows(full_x, full_dy, w_gate, w_up, w_down)
+    out, dx, hidden, dgate, dup = project_rows(full_x, full_dy, w_gate, w_up, w_down)
     gate_grad, up_grad, down_grad, back = reduce_all(
-        flags, grad_g, grad_u, grad_d, out.astype(BF), dx.astype(BF), close
+        counts, full_x, full_dy, dgate, dup, hidden, out, dx, close
     )
-    out_of = (position[:, None] == lanes[None, :]).astype(BF)
+    wide = close.shape[0]
+    lanes = jnp.arange(wide, dtype=jnp.int32)
+    out_of = (position[0][:, None] == lanes[None, :]).astype(BF)
     result = jnp.dot(out_of, back.reshape(wide, 2 * feats), preferred_element_type=F32).astype(BF)
     return result[:, :feats], result[:, feats:], gate_grad, up_grad, down_grad
 

time: 230 us -> 226 us (0.983)
  matrix products: 17.3 us -> 8.38 us
  local copies, waits for them, and re-layouts: 6.17 us -> 10.8 us
    dot_general x5 -> x0, matrix products: 8.48 us -> none  [the longest x1 2.62 us: project_rows(): lax.dot_general(x, dup, over_rows, preferred_element_type=F32).astype(BF)]
    unnamed x13 -> x21, local copies, waits for them, and re-layouts: 4 us -> 8.68 us
    pallas_call x1, Pallas kernels: 95.8 us -> 99.8 us  [reduce_all(): pl.pallas_call(reduce_kernel, out_shape=(out, out, out, back), in_specs=[...]
    pallas_call x1, Pallas kernels: 107 us -> 105 us  [gather_all(): pl.pallas_call(gather_kernel, out_shape=(out, out, out, full, full, close...]
where the time goes in v5:
time: 226 us; the launch traced here: 224 us
  Pallas kernels  204 us (90%)
  local copies, waits for them, and re-layouts  10.8 us (5%)
  matrix products  8.38 us (4%)
    pallas_call x1, Pallas kernels, gather_all(): pl.pallas_call(gather_kernel, out_shape=(out, out, out, full, full, close...  105 us
    pallas_call x1, Pallas kernels, reduce_all(): pl.pallas_call(reduce_kernel, out_shape=(out, out, out, back), in_specs=[...  99.8 us
    unnamed x21, local copies, waits for them, and re-layouts  8.68 us

profile of v5, /device:TPU:16, one launch (start us, length us, event | category | flops | bytes accessed | tf_op | source)
XLA Modules:
  0.0 224.4 jit_solution(14190561165179063919)
XLA Ops:
  0.6 0.7 reshape.29.tags
  1.3 0.7 reshape.30.target
  2.0 0.0 copy-start.1
  2.0 0.9 copy-done.1
  2.9 0.0 copy-start.2
  2.9 0.9 copy-done.2
  3.9 0.0 copy-start.3
  3.9 0.9 copy-done.3
  4.7 0.0 copy-start.4
  4.7 0.9 copy-done.4
  5.6 0.0 copy-start.5
  5.6 0.9 copy-done.5
  6.5 0.0 copy-start.6
  6.5 0.7 copy-done.6
  7.2 104.7 %gather_all.1 = (bf16[2,4,128,1024]{3,2,1,0:T(8,128)(2,1)S(1)}, bf16[2,4,128,1024]{3,2,1,0:T(8,128)(2,1)}, bf16[2,4,128,1024]{3,2,1,0:T(8,128)(2,1)}, bf16[384,1...) custom-call(s32[3]{0:T(128)S(1)} %copy-done.6, ...), custom_call_target="tpu_custom_call" | custom-call | bytes 200000000 | tf_op jit(solution)/shard_map/gather_all/pallas_call | solution.py:339
  111.9 0.0 copy-start
  111.9 0.0 copy-start.7
  111.9 1.0 fusion.6
  112.9 0.0 copy-done
  112.9 0.9 copy-done.7
  113.8 0.0 copy-start.8
  113.8 1.0 fusion.5
  114.8 0.6 copy-done.8
  115.3 1.5 multiply_convert_fusion
  116.9 1.0 fusion.7
  117.9 1.0 add_convert_fusion.dx
  118.9 1.0 convolution_convert_fusion.res
  120.0 99.8 %reduce_all.1 = (f32[3,16,1024]{2,1,0:T(8,128)S(1)}, f32[3,16,1024]{2,1,0:T(8,128)S(1)}, f32[3,16,1024]{2,1,0:T(8,128)S(1)}, bf16[8,8,16,512]{3,2,1,0:T(8,128)(2,1)}) custom-call(s32[3]{0:T(128)S(1)} %copy-done.6, bf16[384,1024]{1,0:T(8,128)(2,1)S(1)} %get-tuple-element.17.xf, bf16[384,1024]{1,0:T(8,128)(2,1)S(1)} %get-tuple-element.18.dyf, ...), custom_call_target="tpu_custom_call" | custom-call | bytes 200000000 | tf_op jit(solution)/shard_map/reduce_all/pallas_call | solution.py:749
  219.7 1.8 fusion.2
  221.6 0.8 fusion.4
  222.3 0.7 copy.16
  223.0 0.7 copy.17
  223.7 0.7 copy.18
  (1 shorter events, 0.0 us)
Async XLA Ops:
  2.0 0.9 copy-start.1
  2.9 0.9 copy-start.2
  3.9 0.9 copy-start.3
  4.7 0.9 copy-start.4
  5.6 0.9 copy-start.5
  6.5 0.7 copy-start.6
  111.9 1.0 copy-start
  111.9 1.9 copy-start.7
  113.8 1.6 copy-start.8

commit v6 on v5

--- a/solution.py
+++ b/solution.py
@@ -93,17 +93,30 @@
 
 
 def gather_kernel(
-    counts, wg, wu, wd, xin, dyin, tags, target, og, ou, od, fx, fdy, close, position, *scratch
+    counts, wg, wu, wd, xhbm, dyhbm, code, og, ou, od, fx, fdy, close, position, *scratch
 ):
     n = len(UNITS)
     zbuf, sbuf = scratch[:n], scratch[n : 2 * n]
-    begins = starts(counts, xin.shape[0])
-    fbuf, fsend, tmid, rows, mine, tok = scratch[2 * n : 2 * n + 6]
-    ys, yr, zs, zr, xs, xr, own, fs, fr, gs, gr, ts, tr, tl, ms, mr, ml = scratch[2 * n + 6 :]
+    begins = starts(counts, xhbm.shape[0])
+    fbuf, fsend, tmid, rows, mine, tok, xin, dyin = scratch[2 * n : 2 * n + 8]
+    ys, yr, zs, zr, xs, xr, own, fs, fr, gs, gr, ts, tr, tl, ms, mr, ml, il = scratch[
+        2 * n + 8 :
+    ]
     p, h, x, z = place()
     at, zline, plane, parts = peers_of(p, h, x, z)
     over = at(1 - h, x, z)
     xline = [at(h, around(x, d, NX), z) for d in range(1, NX)]
+    loads = [pltpu.make_async_copy(xhbm, xin, il.at[0]), pltpu.make_async_copy(dyhbm, dyin, il.at[1])]
+    for c in loads:
+        c.start()
+    placed = {}
+    for u in range(n + 1):
+        w, c0, width = UNITS[u] if u < n else FLIP
+        ours = zbuf[u].at[:, h, rows16(z), :] if u < n else fbuf.at[:, h, x]
+        placed[u] = pltpu.make_async_copy(
+            (wg, wu, wd)[w].at[pl.ds(h, 2), :, pl.ds(c0, width)], ours, il.at[2 + u]
+        )
+        placed[u].start()
     greet(zline + [q for _, q in plane] + [q for _, q in parts])
     weights = (wg, wu, wd)
     outs = (og, ou, od)
@@ -121,9 +134,9 @@
             weights[w].at[pl.ds(1 - h, 2), :, c], theirs, ys.at[u], yr.at[u], over
         )
         sends.append(cross[u])
-        theirs[...] = weights[w][pl.ds(h, 2), :, c]
 
     def first(u):
+        placed[u].wait()
         cross[u].wait_recv()
         v = zbuf[u].at[:, :, rows16(z), :]
         hops = ((2, 2), (3, -2), (0, 1), (1, -1))
@@ -162,6 +175,7 @@
                 waits.append(a)
 
     def flip_first():
+        placed[n].wait()
         cross[n].wait_recv()
         v = fbuf.at[:, :, x]
         near[n] = [remote(v, v, fs.at[d], fr.at[d], xline[d - 1]) for d in (2, 1, 3)]
@@ -191,9 +205,11 @@
         count = xin.shape[0]
         groups = 2 * HALF
         wide = groups * SLOT
-        kind = tags[...]
+        for c in loads:
+            c.wait()
+        kind = code[...] & 3
         base = jnp.where(kind == 0, 0, jnp.where(kind == 1, begins[0], begins[1]))
-        dest = base + target[...]
+        dest = base + lax.shift_right_logical(code[...], 2)
         spread_dest = jnp.broadcast_to(dest.astype(F32), (count, count))
         i = lax.broadcasted_iota(jnp.int32, (count, count), 0)
         j = lax.broadcasted_iota(jnp.int32, (count, count), 1)
@@ -339,7 +355,7 @@
     return pl.pallas_call(
         gather_kernel,
         out_shape=(out, out, out, full, full, close, jax.ShapeDtypeStruct((1, rows), jnp.int32)),
-        in_specs=[pl.BlockSpec(memory_space=pltpu.SMEM)] + [vm] * 7,
+        in_specs=[pl.BlockSpec(memory_space=pltpu.SMEM)] + [hbm] * 5 + [vm],
         out_specs=[hbm] * 5 + [vm] * 2,
         scratch_shapes=[pltpu.VMEM((2, 2, 16 * NZ, u[2]), BF) for u in UNITS]
         + [pltpu.VMEM((4, 2, 16 * NZ, u[2]), BF) for u in UNITS]
@@ -350,6 +366,8 @@
             pltpu.VMEM((2 * NX, NZ, SLOT, 2 * feats), BF),
             pltpu.VMEM((2, rows, feats), BF),
             pltpu.VMEM((2 * NX, NZ, SLOT, 2 * feats), BF),
+            pltpu.VMEM((rows, feats), BF),
+            pltpu.VMEM((rows, feats), BF),
             dma((n + 1,)),
             dma((n + 1,)),
             dma((n, 8)),
@@ -367,13 +385,14 @@
             dma((3, 2)),
             dma((3, 2)),
             dma((2,)),
+            dma((n + 3,)),
         ],
         compiler_params=pltpu.CompilerParams(
-            collective_id=0, has_side_effects=True, vmem_limit_bytes=48 * 1024 * 1024
+            collective_id=0, has_side_effects=True, vmem_limit_bytes=60 * 1024 * 1024
         ),
         cost_estimate=pl.CostEstimate(flops=0, bytes_accessed=200_000_000, transcendentals=0),
         name="gather_all",
-    )(counts, wg, wu, wd, tokens, cotangent, tags.reshape(1, rows), target.reshape(1, rows))
+    )(counts, wg, wu, wd, tokens, cotangent, (target * 4 + tags).reshape(1, rows))
 
 
 def reduce_kernel(

time: 226 us -> 225 us (level)
  local copies, waits for them, and re-layouts: 10.8 us -> 4.23 us
    unnamed x21 -> x17, local copies, waits for them, and re-layouts: 8.68 us -> 2.9 us
where the time goes in v6:
time: 225 us; the launch traced here: 222 us
  Pallas kernels  206 us (92%)
  matrix products  10.4 us (5%)
  local copies, waits for them, and re-layouts  4.23 us (2%)
    pallas_call x1, Pallas kernels, gather_all(): pl.pallas_call(gather_kernel, out_shape=(out, out, out, full, full, close...  106 us
    pallas_call x1, Pallas kernels, reduce_all(): pl.pallas_call(reduce_kernel, out_shape=(out, out, out, back), in_specs=[...  100 us

profile of v6, /device:TPU:16, one launch (start us, length us, event | category | flops | bytes accessed | tf_op | source)
XLA Modules:
  0.0 222.3 jit_solution(16769596452583831070)
XLA Ops:
  0.6 0.7 multiply_add_fusion
  1.4 0.6 reshape.26.code
  1.9 106.1 %gather_all.1 = (bf16[2,4,128,1024]{3,2,1,0:T(8,128)(2,1)}, bf16[2,4,128,1024]{3,2,1,0:T(8,128)(2,1)}, bf16[2,4,128,1024]{3,2,1,0:T(8,128)(2,1)}, bf16[384,1024]...) custom-call(s32[3]{0:T(128)} %counts.3, bf16[3,16,1024]{2,1,0:T(8,128)(2,1)} %wg.1, ...), custom_call_target="tpu_custom_call" | custom-call | bytes 200000000 | tf_op jit(solution)/shard_map/gather_all/pallas_call | solution.py:355
  108.0 0.0 copy-start.1
  108.0 0.0 copy-start.4
  108.1 3.0 %fusion.6 = f32[384,1024]{1,0:T(8,128)S(1)} fusion(bf16[384,1024]{1,0:T(8,128)(2,1)} %get-tuple-element.17.xf, bf16[1024,1024]{1,0:T(8,128)(2,1)} %bitcast.21), kind=kOutput, calls=%fused_computation.14 | convolution fusion | flops 805306368 | bytes 4456448 | tf_op jit(solution)/shard_map/dot_general | solution.py:808
  111.0 0.0 copy-done.1
  111.0 0.0 copy-done.4
  111.0 0.0 copy-start
  111.0 0.0 copy-start.5
  111.1 1.0 fusion.5
  112.1 0.1 copy-done
  112.2 0.7 copy-done.5
  112.9 0.0 copy-start.6
  112.9 1.6 multiply_convert_fusion
  114.4 0.0 copy-done.6
  114.5 1.0 fusion.7
  115.5 1.0 add_convert_fusion.dx
  116.5 0.0 copy-start.2
  116.5 1.0 convolution_convert_fusion.res
  117.6 0.0 copy-done.2
  117.6 0.0 copy-start.3
  117.6 100.0 %reduce_all.1 = (f32[3,16,1024]{2,1,0:T(8,128)S(1)}, f32[3,16,1024]{2,1,0:T(8,128)S(1)}, f32[3,16,1024]{2,1,0:T(8,128)S(1)}, bf16[8,8,16,512]{3,2,1,0:T(8,128)(2,1)}) custom-call(s32[3]{0:T(128)S(1)} %copy-done.2, bf16[384,1024]{1,0:T(8,128)(2,1)S(1)} %copy-done, bf16[384,1024]{1,0:T(8,128)(2,1)S(1)} %copy-done.1, ...), custom_call_target="tpu_custom_call" | custom-call | bytes 200000000 | tf_op jit(solution)/shard_map/reduce_all/pallas_call | solution.py:768
  217.6 0.0 copy-done.3
  217.7 1.8 fusion.2
  219.5 0.8 fusion.4
  220.3 0.7 copy.16
  220.9 0.7 copy.17
  221.6 0.7 copy.18
  (1 shorter events, 0.0 us)
Async XLA Ops:
  108.0 3.0 %copy-start.1 = (bf16[384,1024]{1,0:T(8,128)(2,1)S(1)}, bf16[384,1024]{1,0:T(8,128)(2,1)}, u32[]{:S(2)}) copy-start(bf16[384,1024]{1,0:T(8,128)(2,1)} %get-tuple-element.18.dyf) | copy-start | bytes 2359300
  108.0 3.0 %copy-start.4 = (bf16[2,4,128,1024]{3,2,1,0:T(8,128)(2,1)S(1)}, bf16[2,4,128,1024]{3,2,1,0:T(8,128)(2,1)}, u32[]{:S(2)}) copy-start(bf16[2,4,128,1024]{3,2,1,0:T(8,128)(2,1)} %get-tuple-element.19) | copy-start | bytes 6291460
  111.0 1.1 copy-start
  111.0 1.8 copy-start.5
  112.9 1.6 copy-start.6
  116.5 1.0 copy-start.2
  117.6 100.1 %copy-start.3 = (s32[1,384]{1,0:T(1,128)S(1)}, s32[1,384]{1,0:T(1,128)}, u32[]{:S(2)}) copy-start(s32[1,384]{1,0:T(1,128)} %get-tuple-element.16) | copy-start | bytes 4612

commit v7 on v6

--- a/solution.py
+++ b/solution.py
@@ -12,12 +12,12 @@
 CAP = 12
 SLOT = 16
 UNITS = (
-    (0, 0, 256),
-    (0, 256, 384),
-    (0, 640, 384),
+    (0, 0, 384),
+    (0, 384, 640),
     (1, 0, 512),
     (1, 512, 512),
-    (2, 0, 640),
+    (2, 0, 384),
+    (2, 384, 256),
 )
 FLIP = (2, 640, 384)
 

time: 225 us -> 216 us (0.960); the launches traced: 222 us -> 216 us
  Pallas kernels: 206 us -> 200 us
    pallas_call x1, Pallas kernels: 106 us -> 99.8 us  [gather_all(): pl.pallas_call(gather_kernel, out_shape=(out, out, out, full, full, close...]
where the time goes in v7:
time: 216 us
  Pallas kernels  200 us (93%)
  matrix products  10.4 us (5%)
  local copies, waits for them, and re-layouts  4.24 us (2%)
    pallas_call x1, Pallas kernels, reduce_all(): pl.pallas_call(reduce_kernel, out_shape=(out, out, out, back), in_specs=[...  100 us
    pallas_call x1, Pallas kernels, gather_all(): pl.pallas_call(gather_kernel, out_shape=(out, out, out, full, full, close...  99.8 us

profile of v7, /device:TPU:16, one launch (start us, length us, event | category | flops | bytes accessed | tf_op | source)
XLA Modules:
  0.0 215.9 jit_solution(10950301105762386574)
XLA Ops:
  0.6 0.7 multiply_add_fusion
  1.4 0.6 reshape.26.code
  1.9 99.8 %gather_all.1 = (bf16[2,4,128,1024]{3,2,1,0:T(8,128)(2,1)}, bf16[2,4,128,1024]{3,2,1,0:T(8,128)(2,1)}, bf16[2,4,128,1024]{3,2,1,0:T(8,128)(2,1)}, bf16[384,1024]...) custom-call(s32[3]{0:T(128)} %counts.3, bf16[3,16,1024]{2,1,0:T(8,128)(2,1)} %wg.1, ...), custom_call_target="tpu_custom_call" | custom-call | bytes 200000000 | tf_op jit(solution)/shard_map/gather_all/pallas_call | solution.py:355
  101.7 0.0 copy-start.1
  101.7 0.0 copy-start.4
  101.8 3.0 %fusion.6 = f32[384,1024]{1,0:T(8,128)S(1)} fusion(bf16[384,1024]{1,0:T(8,128)(2,1)} %get-tuple-element.17.xf, bf16[1024,1024]{1,0:T(8,128)(2,1)} %bitcast.21), kind=kOutput, calls=%fused_computation.14 | convolution fusion | flops 805306368 | bytes 4456448 | tf_op jit(solution)/shard_map/dot_general | solution.py:808
  104.7 0.0 copy-done.1
  104.7 0.0 copy-done.4
  104.7 0.0 copy-start
  104.7 0.0 copy-start.5
  104.8 1.0 fusion.5
  105.8 0.1 copy-done
  105.9 0.7 copy-done.5
  106.6 0.0 copy-start.6
  106.6 1.6 multiply_convert_fusion
  108.1 0.0 copy-done.6
  108.2 1.0 fusion.7
  109.2 1.0 add_convert_fusion.dx
  110.2 0.0 copy-start.2
  110.2 1.0 convolution_convert_fusion.res
  111.3 0.0 copy-done.2
  111.3 0.0 copy-start.3
  111.3 100.0 %reduce_all.1 = (f32[3,16,1024]{2,1,0:T(8,128)S(1)}, f32[3,16,1024]{2,1,0:T(8,128)S(1)}, f32[3,16,1024]{2,1,0:T(8,128)S(1)}, bf16[8,8,16,512]{3,2,1,0:T(8,128)(2,1)}) custom-call(s32[3]{0:T(128)S(1)} %copy-done.2, bf16[384,1024]{1,0:T(8,128)(2,1)S(1)} %copy-done, bf16[384,1024]{1,0:T(8,128)(2,1)S(1)} %copy-done.1, ...), custom_call_target="tpu_custom_call" | custom-call | bytes 200000000 | tf_op jit(solution)/shard_map/reduce_all/pallas_call | solution.py:768
  211.3 0.0 copy-done.3
  211.3 1.8 fusion.2
  213.1 0.8 fusion.4
  213.9 0.7 copy.16
  214.6 0.7 copy.17
  215.3 0.7 copy.18
  (1 shorter events, 0.0 us)
Async XLA Ops:
  101.7 3.0 %copy-start.1 = (bf16[384,1024]{1,0:T(8,128)(2,1)S(1)}, bf16[384,1024]{1,0:T(8,128)(2,1)}, u32[]{:S(2)}) copy-start(bf16[384,1024]{1,0:T(8,128)(2,1)} %get-tuple-element.18.dyf) | copy-start | bytes 2359300
  101.7 3.0 %copy-start.4 = (bf16[2,4,128,1024]{3,2,1,0:T(8,128)(2,1)S(1)}, bf16[2,4,128,1024]{3,2,1,0:T(8,128)(2,1)}, u32[]{:S(2)}) copy-start(bf16[2,4,128,1024]{3,2,1,0:T(8,128)(2,1)} %get-tuple-element.19) | copy-start | bytes 6291460
  104.7 1.1 copy-start
  104.7 1.8 copy-start.5
  106.6 1.6 copy-start.6
  110.2 1.0 copy-start.2
  111.3 100.0 %copy-start.3 = (s32[1,384]{1,0:T(1,128)S(1)}, s32[1,384]{1,0:T(1,128)}, u32[]{:S(2)}) copy-start(s32[1,384]{1,0:T(1,128)} %get-tuple-element.16) | copy-start | bytes 4612

commit v8 on v7

--- a/solution.py
+++ b/solution.py
@@ -93,7 +93,7 @@
 
 
 def gather_kernel(
-    counts, wg, wu, wd, xhbm, dyhbm, code, og, ou, od, fx, fdy, close, position, *scratch
+    counts, wg, wu, wd, xhbm, dyhbm, code, og, ou, od, fx, fdy, close, into, *scratch
 ):
     n = len(UNITS)
     zbuf, sbuf = scratch[:n], scratch[n : 2 * n]
@@ -216,16 +216,15 @@
         same = (spread_dest == spread_dest.T) & (i < j)
         slot = jnp.sum(jnp.where(same, 1.0, 0.0), axis=0, keepdims=True)
         place_row = dest * SLOT + slot.astype(jnp.int32)
-        position[...] = place_row
         i = lax.broadcasted_iota(jnp.int32, (wide, count), 0)
-        into = jnp.where(i == place_row, 1.0, 0.0).astype(BF)
+        into[...] = jnp.where(i == place_row, 1.0, 0.0).astype(BF)
         feats = xin.shape[1]
         i = lax.broadcasted_iota(jnp.int32, (groups, count), 0)
         goes = jnp.where(i == dest, 1.0, 0.0).astype(BF)
         sent = jnp.dot(goes, jnp.ones((count, feats), BF), preferred_element_type=F32)
         spot = lax.broadcasted_iota(jnp.int32, (groups, SLOT, feats), 1)
         for b, v in enumerate((xin, dyin)):
-            part = jnp.dot(into, v[...], preferred_element_type=F32)
+            part = jnp.dot(into[...], v[...], preferred_element_type=F32)
             part = part.reshape(groups, SLOT, feats)
             if b == 0:
                 part = jnp.where(spot >= CAP, sent[:, None, :], part)
@@ -354,7 +353,7 @@
     close = jax.ShapeDtypeStruct((2 * HALF * SLOT, rows), BF)
     return pl.pallas_call(
         gather_kernel,
-        out_shape=(out, out, out, full, full, close, jax.ShapeDtypeStruct((1, rows), jnp.int32)),
+        out_shape=(out, out, out, full, full, close, close),
         in_specs=[pl.BlockSpec(memory_space=pltpu.SMEM)] + [hbm] * 5 + [vm],
         out_specs=[hbm] * 5 + [vm] * 2,
         scratch_shapes=[pltpu.VMEM((2, 2, 16 * NZ, u[2]), BF) for u in UNITS]
@@ -821,7 +820,7 @@
 
 def shards(tokens, cotangent, tags, counts, target, gate_weight, up_weight, down_weight):
     feats = tokens.shape[1]
-    w_gate, w_up, w_down, full_x, full_dy, close, position = gather_all(
+    w_gate, w_up, w_down, full_x, full_dy, close, into = gather_all(
         counts, gate_weight, up_weight, down_weight, tokens, cotangent, tags, target
     )
     depth = full_x.shape[1]
@@ -831,9 +830,12 @@
         counts, full_x, full_dy, dgate, dup, hidden, out, dx, close
     )
     wide = close.shape[0]
-    lanes = jnp.arange(wide, dtype=jnp.int32)
-    out_of = (position[0][:, None] == lanes[None, :]).astype(BF)
-    result = jnp.dot(out_of, back.reshape(wide, 2 * feats), preferred_element_type=F32).astype(BF)
+    result = lax.dot_general(
+        into,
+        back.reshape(wide, 2 * feats),
+        (((0,), (0,)), ((), ())),
+        preferred_element_type=F32,
+    ).astype(BF)
     return result[:, :feats], result[:, feats:], gate_grad, up_grad, down_grad
 
 

time: 216 us -> 217 us (level)
  no operation moved by 1% of the time
where the time goes in v8:
time: 217 us
  Pallas kernels  200 us (92%)
  matrix products  10.4 us (5%)
  local copies, waits for them, and re-layouts  4.61 us (2%)
    pallas_call x1, Pallas kernels, reduce_all(): pl.pallas_call(reduce_kernel, out_shape=(out, out, out, back), in_specs=[...  100 us
    pallas_call x1, Pallas kernels, gather_all(): pl.pallas_call(gather_kernel, out_shape=(out, out, out, full, full, close...  100 us

profile of v8, /device:TPU:16, one launch (start us, length us, event | category | flops | bytes accessed | tf_op | source)
XLA Modules:
  0.0 216.6 jit_solution(16438344291109821397)
XLA Ops:
  0.6 0.7 multiply_add_fusion
  1.4 0.6 reshape.25.code
  1.9 100.0 %gather_all.1 = (bf16[2,4,128,1024]{3,2,1,0:T(8,128)(2,1)}, bf16[2,4,128,1024]{3,2,1,0:T(8,128)(2,1)}, bf16[2,4,128,1024]{3,2,1,0:T(8,128)(2,1)}, bf16[384,1024]...) custom-call(s32[3]{0:T(128)} %counts.3, ...), custom_call_target="tpu_custom_call" | custom-call | bytes 200000000 | tf_op jit(solution)/shard_map/gather_all/pallas_call | solution.py:354
  101.9 0.0 copy-start
  101.9 0.0 copy-start.5
  101.9 3.0 %fusion.2 = f32[384,1024]{1,0:T(8,128)S(1)} fusion(bf16[384,1024]{1,0:T(8,128)(2,1)} %get-tuple-element.18.dyf, bf16[1024,1024]{1,0:T(8,128)(2,1)} %bitcast.18), kind=kOutput, calls=%fused_computation.10 | convolution fusion | flops 805306368 | bytes 4456448 | tf_op jit(solution)/shard_map/dot_general | solution.py:813
  104.9 0.0 copy-done
  104.9 0.0 copy-done.5
  104.9 0.0 copy-start.4
  104.9 1.0 fusion.3
  105.9 0.6 copy-done.4
  106.5 1.6 multiply_convert_fusion
  108.0 1.0 fusion.4
  109.1 0.0 copy-start.3
  109.1 1.0 add_convert_fusion.dx
  110.1 0.5 copy-done.3
  110.6 0.0 copy-start.1
  110.6 0.0 copy-start.2
  110.7 1.0 convolution_convert_fusion.res
  111.7 0.1 copy-done.1
  111.8 0.0 copy-done.2
  111.8 0.0 copy-start.6
  111.8 100.2 %reduce_all.1 = (f32[3,16,1024]{2,1,0:T(8,128)S(1)}, f32[3,16,1024]{2,1,0:T(8,128)S(1)}, f32[3,16,1024]{2,1,0:T(8,128)S(1)}, bf16[8,8,16,512]{3,2,1,0:T(8,128)(2,1)}) custom-call(s32[3]{0:T(128)S(1)} %copy-done.2, bf16[384,1024]{1,0:T(8,128)(2,1)S(1)} %copy-done, bf16[384,1024]{1,0:T(8,128)(2,1)S(1)} %copy-done.1, ...), custom_call_target="tpu_custom_call" | custom-call | bytes 200000000 | tf_op jit(solution)/shard_map/reduce_all/pallas_call | solution.py:767
  212.0 0.0 copy-done.6
  212.0 1.8 convolution_convert_fusion.1
  213.8 0.8 fusion.1
  214.6 0.7 copy.16
  215.3 0.7 copy.17
  216.0 0.7 copy.18
Async XLA Ops:
  101.9 3.0 %copy-start = (bf16[384,1024]{1,0:T(8,128)(2,1)S(1)}, bf16[384,1024]{1,0:T(8,128)(2,1)}, u32[]{:S(2)}) copy-start(bf16[384,1024]{1,0:T(8,128)(2,1)} %get-tuple-element.17.xf) | copy-start | bytes 2359300
  101.9 3.0 %copy-start.5 = (bf16[2,4,128,1024]{3,2,1,0:T(8,128)(2,1)S(1)}, bf16[2,4,128,1024]{3,2,1,0:T(8,128)(2,1)}, u32[]{:S(2)}) copy-start(bf16[2,4,128,1024]{3,2,1,0:T(8,128)(2,1)} %get-tuple-element.21) | copy-start | bytes 6291460
  104.9 1.6 copy-start.4
  109.1 1.6 copy-start.3
  110.6 1.1 copy-start.1
  110.6 1.1 copy-start.2
  111.8 100.2 %copy-start.6 = (bf16[1024,384]{1,0:T(8,128)(2,1)S(1)}, bf16[1024,384]{1,0:T(8,128)(2,1)}, u32[]{:S(2)}) copy-start(bf16[1024,384]{1,0:T(8,128)(2,1)} %get-tuple-element.16) | copy-start | bytes 2359300

commit v9 on v8

--- a/solution.py
+++ b/solution.py
@@ -355,7 +355,7 @@
         gather_kernel,
         out_shape=(out, out, out, full, full, close, close),
         in_specs=[pl.BlockSpec(memory_space=pltpu.SMEM)] + [hbm] * 5 + [vm],
-        out_specs=[hbm] * 5 + [vm] * 2,
+        out_specs=[vm] * 7,
         scratch_shapes=[pltpu.VMEM((2, 2, 16 * NZ, u[2]), BF) for u in UNITS]
         + [pltpu.VMEM((4, 2, 16 * NZ, u[2]), BF) for u in UNITS]
         + [
@@ -768,7 +768,7 @@
         reduce_kernel,
         out_shape=(out, out, out, back),
         in_specs=[pl.BlockSpec(memory_space=pltpu.SMEM)] + [vm] * 5 + [hbm] * 2 + [vm],
-        out_specs=[vm] * 3 + [hbm],
+        out_specs=[vm] * 4,
         scratch_shapes=bufs
         + [
             pltpu.VMEM((4, 2, rows, feats), BF),

time: 217 us -> 220 us (1.014)
  Pallas kernels: 200 us -> 203 us
    pallas_call x1, Pallas kernels: 100 us -> 102 us  [gather_all(): pl.pallas_call(gather_kernel, out_shape=(out, out, out, full, full, close...]
where the time goes in v9:
time: 220 us
  Pallas kernels  203 us (92%)
  matrix products  10.4 us (5%)
  local copies, waits for them, and re-layouts  4.61 us (2%)
    pallas_call x1, Pallas kernels, gather_all(): pl.pallas_call(gather_kernel, out_shape=(out, out, out, full, full, close...  102 us
    pallas_call x1, Pallas kernels, reduce_all(): pl.pallas_call(reduce_kernel, out_shape=(out, out, out, back), in_specs=[...  101 us

profile of v9, /device:TPU:16, one launch (start us, length us, event | category | flops | bytes accessed | tf_op | source)
XLA Modules:
  0.0 219.9 jit_solution(9557307329000597073)
XLA Ops:
  0.6 0.7 multiply_add_fusion
  1.4 0.6 reshape.25.code
  1.9 102.2 %gather_all.1 = (bf16[2,4,128,1024]{3,2,1,0:T(8,128)(2,1)}, bf16[2,4,128,1024]{3,2,1,0:T(8,128)(2,1)}, bf16[2,4,128,1024]{3,2,1,0:T(8,128)(2,1)}, bf16[384,1024]...) custom-call(s32[3]{0:T(128)} %counts.3, ...), custom_call_target="tpu_custom_call" | custom-call | bytes 200000000 | tf_op jit(solution)/shard_map/gather_all/pallas_call | solution.py:354
  104.2 0.0 copy-start
  104.2 0.0 copy-start.5
  104.2 3.0 %fusion.2 = f32[384,1024]{1,0:T(8,128)S(1)} fusion(bf16[384,1024]{1,0:T(8,128)(2,1)} %get-tuple-element.18.dyf, bf16[1024,1024]{1,0:T(8,128)(2,1)} %bitcast.18), kind=kOutput, calls=%fused_computation.10 | convolution fusion | flops 805306368 | bytes 4456448 | tf_op jit(solution)/shard_map/dot_general | solution.py:813
  107.1 0.0 copy-done
  107.2 0.0 copy-done.5
  107.2 0.0 copy-start.4
  107.2 1.0 fusion.3
  108.2 0.6 copy-done.4
  108.8 1.5 multiply_convert_fusion
  110.3 1.0 fusion.4
  111.3 0.0 copy-start.3
  111.3 1.0 add_convert_fusion.dx
  112.4 0.5 copy-done.3
  112.9 0.0 copy-start.1
  112.9 0.0 copy-start.2
  112.9 1.0 convolution_convert_fusion.res
  114.0 0.1 copy-done.1
  114.1 0.0 copy-done.2
  114.1 0.0 copy-start.6
  114.1 101.2 %reduce_all.1 = (f32[3,16,1024]{2,1,0:T(8,128)S(1)}, f32[3,16,1024]{2,1,0:T(8,128)S(1)}, f32[3,16,1024]{2,1,0:T(8,128)S(1)}, bf16[8,8,16,512]{3,2,1,0:T(8,128)(2,1)}) custom-call(s32[3]{0:T(128)S(1)} %copy-done.2, bf16[384,1024]{1,0:T(8,128)(2,1)S(1)} %copy-done, bf16[384,1024]{1,0:T(8,128)(2,1)S(1)} %copy-done.1, ...), custom_call_target="tpu_custom_call" | custom-call | bytes 200000000 | tf_op jit(solution)/shard_map/reduce_all/pallas_call | solution.py:767
  215.2 0.0 copy-done.6
  215.2 1.8 convolution_convert_fusion.1
  217.1 0.8 fusion.1
  217.8 0.7 copy.16
  218.5 0.7 copy.17
  219.2 0.7 copy.18
Async XLA Ops:
  104.2 3.0 %copy-start = (bf16[384,1024]{1,0:T(8,128)(2,1)S(1)}, bf16[384,1024]{1,0:T(8,128)(2,1)}, u32[]{:S(2)}) copy-start(bf16[384,1024]{1,0:T(8,128)(2,1)} %get-tuple-element.17.xf) | copy-start | bytes 2359300
  104.2 3.0 %copy-start.5 = (bf16[2,4,128,1024]{3,2,1,0:T(8,128)(2,1)S(1)}, bf16[2,4,128,1024]{3,2,1,0:T(8,128)(2,1)}, u32[]{:S(2)}) copy-start(bf16[2,4,128,1024]{3,2,1,0:T(8,128)(2,1)} %get-tuple-element.21) | copy-start | bytes 6291460
  107.2 1.6 copy-start.4
  111.3 1.6 copy-start.3
  112.9 1.1 copy-start.1
  112.9 1.1 copy-start.2
  114.1 101.2 %copy-start.6 = (bf16[1024,384]{1,0:T(8,128)(2,1)S(1)}, bf16[1024,384]{1,0:T(8,128)(2,1)}, u32[]{:S(2)}) copy-start(bf16[1024,384]{1,0:T(8,128)(2,1)} %get-tuple-element.16) | copy-start | bytes 2359300
